TPU v7x, 32 devices: a whole 2x2x4 slice. The times are simulated.
32 devices in a mesh: segment: 2 (over core), dp: 8 (over z, x), mp: 2 (over y).
Axes of the slice: x: 2, y: 2, z: 4, core: 2. Of those that a mesh axis runs over, the one named last changes fastest.
Arguments:
- grad_top: bfloat16 [4096, 2048], P('dp'), may hold values from -6 to 6
- saved_query: bfloat16 [2, 4096, 2048], P('segment', 'dp', 'mp'), may hold values from -12 to 12
- saved_key: bfloat16 [2, 6144, 2048], P('segment', 'dp', 'mp'), may hold values from -4 to 4
- saved_value: bfloat16 [2, 6144, 2048], P('segment', 'dp', 'mp'), may hold values from -6 to 6
- w_query: bfloat16 [2, 2048, 2048], P('segment', 'mp', 'dp'), may hold values from -0.125 to 0.125
- w_key: bfloat16 [2, 2048, 2048], P('segment', 'mp', 'dp'), may hold values from -0.125 to 0.125
- w_value: bfloat16 [2, 2048, 2048], P('segment', 'mp', 'dp'), may hold values from -0.125 to 0.125
- w_out: bfloat16 [2, 2048, 2048], P('segment', 'mp', 'dp'), may hold values from -0.125 to 0.125
- query_length: int32 [16, 2], P('dp'), may hold values from 64 to 128
- key_offset: int32 [16, 2], P('dp'), may hold values from 0 to 2, as said below
- key_length: int32 [16, 2], P('dp'), may hold values from 64 to 256
- tile_owner: int32 [16, 3], replicated, may hold values from 0 to 47, as said below
Outputs:
- section_grads: bfloat16 [2, 4096, 2048], P('segment', 'dp', 'mp')
- encoder_grads: bfloat16 [6144, 2048], P('dp', ('segment', 'mp'))
Inputs may be any that keep to these rules, and one draw needn't show every extreme that they name: Example 0 takes tiles 0 to key_offset[s, 1] - 1 and example 1 the rest of the sequence's encoder tiles; each example holds at least one tile and its rows fit in its tiles. `tile_owner`: every global tile appears once. Tile t is owned by dp index t // 6; the owner of a tile of dp index i (sequences i * 2 to i * 2 + 1) is i - 1, i or i + 1, wrapping around. Each dp index hands 1 to 2 tiles to each neighbour, and 2 is reached in every draw.
All inputs are finite; a program needn't handle non-finite values.
Results may differ from a plain program's by a relative error of at most 0.019.
Values may be sent and summed in bfloat16 or wider, within the bound.
A program may use at most 128 MiB of HBM per device.

v0:
```python
import jax
import jax.numpy as jnp
from jax import lax
from jax.sharding import PartitionSpec as P

DH = 256
TILE = 128
CAP = 2


masked_floor = -1e30


def shifted(block, axis, distance):
    devices = range(lax.axis_size(axis))
    route = [(i - distance, i) for i in devices if i - distance in devices]
    return lax.ppermute(block, axis, route)


def extended_2(block, sides, width):
    for axis, dim in sides:
        count = lax.axis_size(axis)
        forward = [(i, i + 1) for i in range(count - 1)]
        forward.append((count - 1, 0))
        backward = [(target, source) for source, target in forward]
        low = lax.ppermute(
            lax.slice_in_dim(block, block.shape[dim] - width, None, axis=dim), axis, forward
        )
        high = lax.ppermute(lax.slice_in_dim(block, 0, width, axis=dim), axis, backward)
        block = jnp.concatenate([low, block, high], axis=dim)
    return block


def example_mask(query_length, key_offset, key_length, q_rows, k_rows):
    row_ids = jnp.arange(q_rows, dtype=jnp.int32)[:, None]
    starts = jnp.arange(query_length.shape[0], dtype=jnp.int32)[None, :] * TILE
    inside_q = (row_ids >= starts) & (row_ids < starts + query_length[None, :])
    col_ids = jnp.arange(k_rows, dtype=jnp.int32)[:, None]
    key_start = key_offset[None, :] * TILE
    inside_k = (col_ids >= key_start) & (col_ids < key_start + key_length[None, :])
    return jnp.any(inside_q[:, None, :] & inside_k[None, :, :], axis=-1)


def sequence_backward(operands, query_full, out_full):
    grad_in, query_block, key_block, value_block, query_length, key_offset, key_length = operands
    q_rows, local_width = query_block.shape
    k_rows = key_block.shape[0]
    head_count = local_width // DH
    score_scale = DH ** (-0.5)
    out_grad = lax.dot_general(
        grad_in, out_full, (((1,), (1,)), ((), ())), preferred_element_type=jnp.float32
    ).astype(jnp.bfloat16)
    q_heads = query_block.reshape(q_rows, head_count, DH)
    k_heads = key_block.reshape(k_rows, head_count, DH)
    v_heads = value_block.reshape(k_rows, head_count, DH)
    grad_heads = out_grad.reshape(q_rows, head_count, DH)
    scores = (
        jnp.einsum("qhd,khd->hqk", q_heads, k_heads, preferred_element_type=jnp.float32)
        * score_scale
    )
    allowed = example_mask(query_length, key_offset, key_length, q_rows, k_rows)[None]
    masked = jnp.where(allowed, scores, masked_floor)
    row_max = jnp.max(masked, axis=-1, keepdims=True)
    exp_terms = jnp.where(allowed, jnp.exp(masked - row_max), 0.0)
    denominator = jnp.maximum(jnp.sum(exp_terms, axis=-1, keepdims=True), 1.0)
    attention_probs = exp_terms / denominator
    prob_bf = attention_probs.astype(jnp.bfloat16)
    attended = jnp.einsum("hqk,khd->qhd", prob_bf, v_heads, preferred_element_type=jnp.float32)
    out_dot = jnp.sum(grad_heads.astype(jnp.float32) * attended, axis=-1)
    prob_grad = jnp.einsum("qhd,khd->hqk", grad_heads, v_heads, preferred_element_type=jnp.float32)
    score_grad = (attention_probs * (prob_grad - jnp.transpose(out_dot)[:, :, None])).astype(
        jnp.bfloat16
    )
    query_grad = (
        jnp.einsum("hqk,khd->qhd", score_grad, k_heads, preferred_element_type=jnp.float32)
        * score_scale
    ).astype(jnp.bfloat16)
    key_gradient = (
        jnp.einsum("hqk,qhd->khd", score_grad, q_heads, preferred_element_type=jnp.float32)
        * score_scale
    ).astype(jnp.bfloat16)
    value_grad = jnp.einsum(
        "hqk,qhd->khd", prob_bf, grad_heads, preferred_element_type=jnp.float32
    ).astype(jnp.bfloat16)
    mixed_grad = jnp.dot(
        query_grad.reshape(q_rows, local_width), query_full, preferred_element_type=jnp.float32
    )
    return (
        mixed_grad,
        key_gradient.reshape(k_rows, local_width),
        value_grad.reshape(k_rows, local_width),
    )


def ranked(marked):
    return jnp.cumsum(marked.astype(jnp.int32)) - 1


def on_device(
    grad_top,
    saved_query,
    saved_key,
    saved_value,
    w_query,
    w_key,
    w_value,
    w_out,
    query_length,
    key_offset,
    key_length,
    tile_owner,
):
    segment_count = lax.axis_size("segment")
    segment_id = lax.axis_index("segment")
    micro_count = query_length.shape[0]
    q_rows = grad_top.shape[0] // micro_count
    k_rows = saved_key.shape[1] // micro_count
    width = grad_top.shape[1]
    local_width = saved_query.shape[2]
    half_width = width // lax.axis_size("mp")
    out_full, query_full, key_full, complete_value = (
        lax.all_gather(w_out[0], "dp", axis=1, tiled=True),
        lax.all_gather(w_query[0], "dp", axis=1, tiled=True),
        lax.all_gather(w_key[0], "dp", axis=1, tiled=True),
        lax.all_gather(w_value[0], "dp", axis=1, tiled=True),
    )

    def run_layer(operands):
        return sequence_backward(operands, query_full, out_full)

    def bypass_layer(operands):
        return (
            jnp.zeros((q_rows, width), jnp.float32),
            jnp.zeros((k_rows, local_width), jnp.bfloat16),
            jnp.zeros((k_rows, local_width), jnp.bfloat16),
        )

    incoming = jnp.zeros((q_rows, width), jnp.bfloat16)
    sections = jnp.zeros((micro_count * q_rows, half_width), jnp.bfloat16)
    key_grads = jnp.zeros((micro_count * k_rows, local_width), jnp.bfloat16)
    value_grads = jnp.zeros((micro_count * k_rows, local_width), jnp.bfloat16)
    for clock_tick in range(micro_count + 1):
        step_id = clock_tick - 1 + segment_id
        active = (step_id >= 0) & (step_id < micro_count)
        picked = jnp.clip(step_id, 0, micro_count - 1)
        top_rows = lax.dynamic_slice_in_dim(grad_top, picked * q_rows, q_rows, 0)
        grad_in = jnp.where(segment_id == segment_count - 1, top_rows, incoming)
        query_block = lax.dynamic_slice_in_dim(saved_query[0], picked * q_rows, q_rows, 0)
        key_block = lax.dynamic_slice_in_dim(saved_key[0], picked * k_rows, k_rows, 0)
        value_block = lax.dynamic_slice_in_dim(saved_value[0], picked * k_rows, k_rows, 0)
        lengths_q = lax.dynamic_index_in_dim(query_length, picked, 0, keepdims=False)
        offsets_k = lax.dynamic_index_in_dim(key_offset, picked, 0, keepdims=False)
        lengths_k = lax.dynamic_index_in_dim(key_length, picked, 0, keepdims=False)
        mixed_grad, key_gradient, value_grad = lax.cond(
            active,
            run_layer,
            bypass_layer,
            (grad_in, query_block, key_block, value_block, lengths_q, offsets_k, lengths_k),
        )
        summed_share = lax.psum_scatter(
            mixed_grad.astype(jnp.bfloat16), "mp", scatter_dimension=1, tiled=True
        ).astype(jnp.float32)
        own_input = lax.dynamic_slice_in_dim(
            grad_in, lax.axis_index("mp") * half_width, half_width, 1
        )
        own_section = (own_input.astype(jnp.float32) + summed_share).astype(jnp.bfloat16)
        if clock_tick < micro_count:
            full_section = lax.all_gather(own_section, "mp", axis=1, tiled=True)
        sections = jnp.where(
            active,
            lax.dynamic_update_slice_in_dim(sections, own_section, picked * q_rows, 0),
            sections,
        )
        key_grads = jnp.where(
            active,
            lax.dynamic_update_slice_in_dim(key_grads, key_gradient, picked * k_rows, 0),
            key_grads,
        )
        value_grads = jnp.where(
            active,
            lax.dynamic_update_slice_in_dim(value_grads, value_grad, picked * k_rows, 0),
            value_grads,
        )
        if clock_tick < micro_count:
            incoming = shifted(full_section, "segment", -1)
    encoder_partial = jnp.dot(key_grads, key_full, preferred_element_type=jnp.float32) + jnp.dot(
        value_grads, complete_value, preferred_element_type=jnp.float32
    )
    reduced = lax.psum_scatter(
        encoder_partial.astype(jnp.bfloat16), ("segment", "mp"), scatter_dimension=1, tiled=True
    )
    tiles_dev = reduced.shape[0] // TILE
    features = reduced.shape[1]
    local_tiles = reduced.reshape(tiles_dev, TILE, features)
    devices = lax.axis_size("dp")
    my_index = lax.axis_index("dp")
    owners_all = tile_owner.reshape(devices, tiles_dev)

    def route_plan(source):
        owner_row = lax.dynamic_index_in_dim(owners_all, source % devices, 0, keepdims=False)
        owner_step = (owner_row // tiles_dev - source % devices + devices) % devices
        return (owner_step, owner_row % tiles_dev)

    mine_step, mine_slot = route_plan(my_index)
    left_step, left_slot = route_plan(my_index - 1 + devices)
    right_step, right_slot = route_plan(my_index + 1)
    capacity_ids = jnp.arange(CAP, dtype=jnp.int32)[:, None]
    to_left = mine_step == devices - 1
    rightward_send = mine_step == 1
    pick_left = (ranked(to_left)[None, :] == capacity_ids) & to_left[None, :]
    pick_right = (ranked(rightward_send)[None, :] == capacity_ids) & rightward_send[None, :]
    selector_mask = jnp.concatenate([pick_left, pick_right], axis=0).astype(jnp.bfloat16)
    outgoing = jnp.einsum(
        "sa,ayk->syk", selector_mask, local_tiles, preferred_element_type=jnp.float32
    ).astype(jnp.bfloat16)
    outgoing = outgoing.reshape(2 * CAP * TILE, features)
    extended = extended_2(outgoing, (("dp", 0),), CAP * TILE)
    from_left = extended[: CAP * TILE].reshape(CAP, TILE, features)
    from_right = extended[extended.shape[0] - CAP * TILE :].reshape(CAP, TILE, features)
    candidates = jnp.concatenate([from_left, local_tiles, from_right], axis=0)
    left_marked = left_step == 1
    left_hit = (ranked(left_marked)[None, :] == capacity_ids) & left_marked[None, :]
    left_target = jnp.sum(jnp.where(left_hit, left_slot[None, :], 0), axis=1)
    right_marked = right_step == devices - 1
    right_hit = (ranked(right_marked)[None, :] == capacity_ids) & right_marked[None, :]
    right_target = jnp.sum(jnp.where(right_hit, right_slot[None, :], 0), axis=1)
    target = jnp.concatenate([left_target, mine_slot, right_target])
    usable = jnp.concatenate(
        [jnp.any(left_hit, axis=1), mine_step == 0, jnp.any(right_hit, axis=1)]
    )
    placer = (
        (jnp.arange(tiles_dev, dtype=jnp.int32)[:, None] == target[None, :]) & usable[None, :]
    ).astype(jnp.bfloat16)
    owned_rows = jnp.einsum(
        "sc,crf->srf", placer, candidates, preferred_element_type=jnp.float32
    ).astype(jnp.bfloat16)
    return (sections[None], owned_rows.reshape(tiles_dev * TILE, features))


def solution(mesh):
    in_specs = (
        P("dp", None),
        P("segment", "dp", "mp"),
        P("segment", "dp", "mp"),
        P("segment", "dp", "mp"),
        P("segment", "mp", "dp"),
        P("segment", "mp", "dp"),
        P("segment", "mp", "dp"),
        P("segment", "mp", "dp"),
        P("dp", None),
        P("dp", None),
        P("dp", None),
        P(),
    )
    out_specs = (P("segment", "dp", "mp"), P("dp", ("segment", "mp")))
    return jax.shard_map(
        on_device, mesh=mesh, in_specs=in_specs, out_specs=out_specs, check_vma=False
    )
```

profile of v0, /device:TPU:0, one launch (start us, length us, event | category | flops | bytes accessed | tf_op | source)
XLA Modules:
  0.0 555.2 jit_solution(11707310913632669811)
XLA Ops:
  8.8 2.5 dynamic-slice_select_fusion.2
  11.2 76.6 %all-gather.15.cloned.1.call-done = bf16[1,1024,2048]{2,1,0:T(8,128)(2,1)} async-done(((bf16[1,1024,256]{2,1,0:T(8,128)(2,1)}), bf16[1,1024,2048]{2,1,0:T(8,128)(2,1)}) %all-gather.15.cloned.1.call-update) | async-done | bytes 4194320 | tf_op jit(solution)/shard_map/all_gather | solution.py:122
  87.8 75.3 %all-gather.17.cloned.1.call-done = bf16[1,1024,2048]{2,1,0:T(8,128)(2,1)} async-done(((bf16[1,1024,256]{2,1,0:T(8,128)(2,1)}), bf16[1,1024,2048]{2,1,0:T(8,128)(2,1)}) %all-gather.17.cloned.1.call-update) | async-done | bytes 4194320 | tf_op jit(solution)/shard_map/all_gather | solution.py:123
  163.1 3.0 conditional.3
  166.3 46.4 %reduce-scatter.5.cloned.1.call-done = bf16[256,1024]{1,0:T(8,128)(2,1)} async-done(((bf16[256,2048]{1,0:T(8,128)(2,1)}), bf16[256,1024]{1,0:T(8,128)(2,1)}) %reduce-scatter.5.cloned.1.call-update) | async-done | bytes 524304 | tf_op jit(solution)/shard_map/reduce_scatter | solution.py:160
  213.8 2.4 select_dynamic-update-slice_fusion.7
  216.3 21.4 %all-gather.11.cloned.1.call-done = bf16[256,2048]{1,0:T(8,128)(2,1)} async-done(((bf16[256,1024]{1,0:T(8,128)(2,1)}), bf16[256,2048]{1,0:T(8,128)(2,1)}) %all-gather.11.cloned.1.call-update) | async-done | bytes 1048592 | tf_op jit(solution)/shard_map/all_gather | solution.py:168
  237.7 1.5 collective-permute-start
  239.1 3.4 collective-permute-done
  242.6 3.0 dynamic-slice_select_fusion.1
  245.5 31.3 %conditional.4 = (bf16[256,2048]{1,0:T(8,128)(2,1)}, bf16[384,1024]{0,1:T(8,128)(2,1)}, bf16[384,1024]{0,1:T(8,128)(2,1)}) conditional(s32[]{:T(128)} %convert_element_type.214, () %tuple.46, (s32[2,2]{1,0:T(2,128)S(1)}, s32[]{:T(128)}, s32[2,2]{1,0:T(2,128)S(1)}, s32[2,2]{1,0:T(2,128)S(1)}, bf16[1,512,1024]{2,1,0:T(8,128)(2,1)}, ...), branch_computations={%region_7.8_spmd, %region_8.13_spmd} | conditional | flops 3363606528 | bytes 75467568 | solution.py:154
  245.8 1.6 copy.92
  247.4 1.6 copy.93
  249.0 3.5 constant_dynamic-slice_fusion.6
  252.5 2.3 copy.91
  254.8 2.2 constant_dynamic-slice_fusion.8
  257.0 3.4 fusion.94
  260.4 4.6 convolution_convert_fusion.3
  265.0 2.0 copy.115
  267.0 2.5 fusion.21
  273.0 2.3 fusion.98
  275.4 1.4 convolution_convert_fusion.2
  276.9 20.4 %reduce-scatter.7.cloned.1.call-done = bf16[256,1024]{1,0:T(8,128)(2,1)} async-done(((bf16[256,2048]{1,0:T(8,128)(2,1)}), bf16[256,1024]{1,0:T(8,128)(2,1)}) %reduce-scatter.7.cloned.1.call-update) | async-done | bytes 524304 | tf_op jit(solution)/shard_map/reduce_scatter | solution.py:160
  297.3 2.7 select_dynamic-update-slice_fusion.6
  301.5 19.9 %all-gather.13.cloned.1.call-done = bf16[256,2048]{1,0:T(8,128)(2,1)} async-done(((bf16[256,1024]{1,0:T(8,128)(2,1)}), bf16[256,2048]{1,0:T(8,128)(2,1)}) %all-gather.13.cloned.1.call-update) | async-done | bytes 1048592 | tf_op jit(solution)/shard_map/all_gather | solution.py:168
  327.4 2.5 select_dynamic-update-slice_fusion.1
  329.9 2.8 select_dynamic-update-slice_fusion.4
  332.6 1.4 dynamic-slice_select_fusion
  334.1 23.1 %conditional.5 = (bf16[256,2048]{1,0:T(8,128)(2,1)}, bf16[384,1024]{0,1:T(8,128)(2,1)}, bf16[384,1024]{0,1:T(8,128)(2,1)}) conditional(s32[]{:T(128)} %convert_element_type.219, () %tuple.48, (s32[2,2]{1,0:T(2,128)S(1)}, s32[]{:T(128)}, s32[2,2]{1,0:T(2,128)S(1)}, s32[2,2]{1,0:T(2,128)S(1)}, bf16[1,512,1024]{2,1,0:T(8,128)(2,1)}, ...), branch_computations={%region_14.15_spmd, %region_15.20_spmd} | conditional | flops 3363606528 | bytes 85953360 | solution.py:154
  334.6 1.6 copy.95
  336.2 1.6 copy.96
  337.8 3.1 constant_dynamic-slice_fusion.12
  342.1 2.1 fusion.95
  344.2 3.5 convolution_convert_fusion.5
  347.9 2.3 fusion.38
  353.3 2.2 fusion.99
  355.5 1.4 convolution_convert_fusion.4
  357.2 3.5 select_dynamic-update-slice_fusion
  360.7 37.8 %all-gather.21.cloned.1.call-done = bf16[1,1024,2048]{2,1,0:T(8,128)(2,1)} async-done(((bf16[1,1024,256]{2,1,0:T(8,128)(2,1)}), bf16[1,1024,2048]{2,1,0:T(8,128)(2,1)}) %all-gather.21.cloned.1.call-update) | async-done | bytes 4194320 | tf_op jit(solution)/shard_map/all_gather | solution.py:125
  398.5 8.8 %fusion.51 = f32[768,2048]{1,0:T(8,128)} fusion(bf16[768,1024]{0,1:T(8,128)(2,1)} %get-tuple-element.478, bf16[1,1024,2048]{2,1,0:T(8,128)(2,1)} %all-gather.21.cloned.1.call-done), kind=kOutput, calls=%fused_computation.106 | convolution fusion | flops 3221225472 | bytes 12058624 | tf_op jit(solution)/shard_map/dot_general | solution.py:186
  407.3 66.5 %all-gather.19.cloned.1.call-done = bf16[1,1024,2048]{2,1,0:T(8,128)(2,1)} async-done(((bf16[1,1024,256]{2,1,0:T(8,128)(2,1)}), bf16[1,1024,2048]{2,1,0:T(8,128)(2,1)}) %all-gather.19.cloned.1.call-update) | async-done | bytes 4194320 | tf_op jit(solution)/shard_map/all_gather | solution.py:124
  473.8 9.6 %add_convert_fusion = bf16[768,2048]{1,0:T(8,128)(2,1)} fusion(f32[768,2048]{1,0:T(8,128)} %fusion.51, bf16[768,1024]{0,1:T(8,128)(2,1)} %get-tuple-element.479, bf16[1,1024,2048]{2,1,0:T(8,128)(2,1)} %all-gather.19.cloned.1.call-done), kind=kOutput, calls=%fused_computation.105 | convolution fusion | flops 3224371200 | bytes 15204352 | tf_op jit(solution)/shard_map/dot_general | solution.py:186
  485.6 34.2 %reduce-scatter.11.cloned.1.call-done = bf16[768,512]{1,0:T(8,128)(2,1)} async-done(((bf16[768,2048]{1,0:T(8,128)(2,1)}), bf16[768,512]{1,0:T(8,128)(2,1)}) %reduce-scatter.11.cloned.1.call-update) | async-done | bytes 786448 | tf_op jit(solution)/shard_map/reduce_scatter | solution.py:189
  519.7 1.7 convolution_convert_fusion.6
  521.9 1.5 collective-permute-start.2
  524.2 3.3 collective-permute-start.3
  528.9 13.4 %reduce-scatter.9.cloned.1.call-done = bf16[256,1024]{1,0:T(8,128)(2,1)} async-done(((bf16[256,2048]{1,0:T(8,128)(2,1)}), bf16[256,1024]{1,0:T(8,128)(2,1)}) %reduce-scatter.9.cloned.1.call-update) | async-done | bytes 524304 | tf_op jit(solution)/shard_map/reduce_scatter | solution.py:160
  542.3 1.5 fusion.68
  (132 shorter events, 30.5 us)
Async XLA Ops:
  7.2 156.0 %copy-start = (bf16[1,768,1024]{2,1,0:T(8,128)(2,1)S(1)}, bf16[1,768,1024]{2,1,0:T(8,128)(2,1)}, u32[]{:S(2)}) copy-start(bf16[1,768,1024]{2,1,0:T(8,128)(2,1)} %param.20) | copy-start | bytes 4718596
  7.2 156.0 %copy-start.1 = (bf16[1,768,1024]{2,1,0:T(8,128)(2,1)S(1)}, bf16[1,768,1024]{2,1,0:T(8,128)(2,1)}, u32[]{:S(2)}) copy-start(bf16[1,768,1024]{2,1,0:T(8,128)(2,1)} %param.21) | copy-start | bytes 4718596
  7.2 155.9 %copy-start.19 = (s32[2,2]{1,0:T(2,128)S(1)}, s32[2,2]{1,0:T(2,128)}, u32[]{:S(2)}) copy-start(s32[2,2]{1,0:T(2,128)} %param.26) | copy-start | bytes 52
  7.2 155.9 %copy-start.20 = (s32[2,2]{1,0:T(2,128)S(1)}, s32[2,2]{1,0:T(2,128)}, u32[]{:S(2)}) copy-start(s32[2,2]{1,0:T(2,128)} %param.27) | copy-start | bytes 52
  7.2 155.9 %copy-start.21 = (s32[2,2]{1,0:T(2,128)S(1)}, s32[2,2]{1,0:T(2,128)}, u32[]{:S(2)}) copy-start(s32[2,2]{1,0:T(2,128)} %param.28) | copy-start | bytes 52
  7.2 80.6 %all-gather.15.cloned.1.call-start = ((), (), s32[]{:S(2)}) async-start(), calls=%async_computation.10 | async-start | bytes 4718592 | tf_op jit(solution)/shard_map/all_gather | solution.py:122
  7.9 155.2 %all-gather.17.cloned.1.call-start = ((), (), s32[]{:S(2)}) async-start(), calls=%async_computation.11 | async-start | bytes 4718592 | tf_op jit(solution)/shard_map/all_gather | solution.py:123
  8.7 204.0 %reduce-scatter.5.cloned.1.call-start = ((), (), s32[]{:S(2)}) async-start(), calls=%async_computation.4 | async-start | bytes 1572864 | tf_op jit(solution)/shard_map/reduce_scatter | solution.py:160
  166.2 71.5 %all-gather.11.cloned.1.call-start = ((), (), s32[]{:S(2)}) async-start(), calls=%async_computation.5 | async-start | bytes 1572864 | tf_op jit(solution)/shard_map/all_gather | solution.py:168
  216.2 81.1 %reduce-scatter.7.cloned.1.call-start = ((), (), s32[]{:S(2)}) async-start(), calls=%async_computation.6 | async-start | bytes 1572864 | tf_op jit(solution)/shard_map/reduce_scatter | solution.py:160
  237.7 4.9 collective-permute-start
  267.0 2.5 copy-start.15
  267.0 2.5 copy-start.18
  267.0 2.7 copy-start.27
  269.7 1.0 copy-start.12
  269.7 3.3 copy-start.24
  270.7 1.8 copy-start.7
  276.8 44.6 %all-gather.13.cloned.1.call-start = ((), (), s32[]{:S(2)}) async-start(), calls=%async_computation.7 | async-start | bytes 1572864 | tf_op jit(solution)/shard_map/all_gather | solution.py:168
  300.0 98.6 %all-gather.21.cloned.1.call-start = ((), (), s32[]{:S(2)}) async-start(), calls=%async_computation.13 | async-start | bytes 4718592 | tf_op jit(solution)/shard_map/all_gather | solution.py:125
  300.7 173.1 %all-gather.19.cloned.1.call-start = ((), (), s32[]{:S(2)}) async-start(), calls=%async_computation.12 | async-start | bytes 4718592 | tf_op jit(solution)/shard_map/all_gather | solution.py:124
  301.5 218.3 %reduce-scatter.11.cloned.1.call-start = ((), (), s32[]{:S(2)}) async-start(), calls=%async_computation.9 | async-start | bytes 3932160 | tf_op jit(solution)/shard_map/reduce_scatter | solution.py:189
  321.4 11.2 %collective-permute-start.1 = (bf16[256,2048]{1,0:T(8,128)(2,1)}, bf16[256,2048]{1,0:T(8,128)(2,1)S(1)}, u32[]{:S(2)}, u32[]{:S(2)}) collective-permute-start(bf16[256,2048]{1,0:T(8,128)(2,1)} %all-gather.13.cloned.1.call-done), channel_id=1, source_target_pairs={{16,0},{17,1},{18,2},{19,3},{20,4},{21,5},{22,6},{23,7},{24,8},{25... | collective-permute-start | bytes 3145736 | tf_op jit(solution)/shard_map/ppermute | solution.py:17
  329.9 2.8 copy-start.3
  336.2 1.6 copy-start.5
  337.8 3.1 copy-start.2
  341.0 1.1 copy-start.8
  342.1 2.1 copy-start.10
  347.8 2.4 copy-start.16
  347.9 2.4 copy-start.28
  350.8 2.5 copy-start.25
  483.4 0.7 copy-start.22
  483.4 58.9 %reduce-scatter.9.cloned.1.call-start = ((), (), s32[]{:S(2)}) async-start(), calls=%async_computation.8 | async-start | bytes 1572864 | tf_op jit(solution)/shard_map/reduce_scatter | solution.py:160
  521.9 20.4 %copy-start.9 = (bf16[256,2048]{1,0:T(8,128)(2,1)S(1)}, bf16[256,2048]{1,0:T(8,128)(2,1)}, u32[]{:S(2)}) copy-start(bf16[256,2048]{1,0:T(8,128)(2,1)} %dynamic-slice_select_fusion) | copy-start | bytes 3145732
  521.9 22.3 %collective-permute-start.2 = (bf16[256,512]{1,0:T(8,128)(2,1)S(1)}, bf16[256,512]{1,0:T(8,128)(2,1)S(1)}, u32[]{:S(2)}, u32[]{:S(2)}) collective-permute-start(bf16[256,512]{1,0:T(8,128)(2,1)S(1)} %bitcast.243), channel_id=1, source_target_pairs={{0,2},{2,4},{4,6},{6,8},{8,10},{10,12},{12,14},{14,0},{1,3},{3,5},... | collective-permute-start | bytes 786440 | tf_op jit(solution)/shard_map/ppermute | solution.py:26
  524.2 20.4 %collective-permute-start.3 = (bf16[256,512]{1,0:T(8,128)(2,1)}, bf16[256,512]{1,0:T(8,128)(2,1)}, u32[]{:S(2)}, u32[]{:S(2)}) collective-permute-start(bf16[256,512]{1,0:T(8,128)(2,1)} %bitcast.70), channel_id=1, source_target_pairs={{2,0},{4,2},{6,4},{8,6},{10,8},{12,10},{14,12},{0,14},{3,1},{5,3},... | collective-permute-start | bytes 786440 | tf_op jit(solution)/shard_map/ppermute | solution.py:29
  528.9 14.9 %copy-start.4 = (bf16[768,512]{1,0:T(8,128)(2,1)S(1)}, bf16[768,512]{1,0:T(8,128)(2,1)}, u32[]{:S(2)}) copy-start(bf16[768,512]{1,0:T(8,128)(2,1)} %reduce-scatter.11.cloned.1.call-done) | copy-start | bytes 2359300
  543.8 3.0 copy-start.13
Sparse Core Ops, SparseCore 0:
  10.1 77.7 all-gather.14
  89.9 73.1 all-gather.16
  166.3 46.3 reduce-scatter.4
  216.3 21.2 all-gather.10
  276.9 20.3 reduce-scatter.6
  300.1 21.2 all-gather.12
  323.5 75.0 all-gather.20
  400.6 73.1 all-gather.18
  483.6 36.1 reduce-scatter.10
  521.9 20.3 reduce-scatter.8
where the time goes:
time: 562 us; the launch traced here: 555 us
  waiting for transfers between devices  418 us (74%)
  matrix products  51.6 us (9%)
  local copies, waits for them, and re-layouts  35.7 us (6%)
  other arithmetic  26.2 us (5%)
  between operations  14.9 us (3%)
  starting transfers between devices  7.91 us (1%)
    reduce_scatter x3, waiting for transfers between devices, on_device(): lax.psum_scatter(mixed_grad.astype(jnp.bfloat16), 'mp', scatter_dimension...  80.3 us
    all_gather x1, waiting for transfers between devices, on_device(): lax.all_gather(w_out[0], 'dp', axis=1, tiled=True)  76.6 us
    all_gather x1, waiting for transfers between devices, on_device(): lax.all_gather(w_query[0], 'dp', axis=1, tiled=True)  75.3 us
    all_gather x1, waiting for transfers between devices, on_device(): lax.all_gather(w_key[0], 'dp', axis=1, tiled=True)  66.5 us
    all_gather x2, waiting for transfers between devices, on_device(): full_section = lax.all_gather(own_section, 'mp', axis=1, tiled=True)  41.3 us
    all_gather x1, waiting for transfers between devices, on_device(): lax.all_gather(w_value[0], 'dp', axis=1, tiled=True)  37.8 us
    reduce_scatter x1, waiting for transfers between devices, on_device(): lax.psum_scatter(encoder_partial.astype(jnp.bfloat16), ('segment', 'mp'),...  34.2 us
    another operation x11, local copies, waits for them, and re-layouts  14.8 us
  transfers between devices with their start and end apart: 14, of which 11 were waited for; matrix products, arithmetic and copies ran while one was open for 10% of the time, Pallas kernels for 0%

commit v1 on v0

--- a/solution.py
+++ b/solution.py
@@ -93,7 +93,9 @@
 
 
 def ranked(marked):
-    return jnp.cumsum(marked.astype(jnp.int32)) - 1
+    ids = jnp.arange(marked.shape[0], dtype=jnp.int32)
+    upto = ids[None, :] <= ids[:, None]
+    return jnp.sum((upto & marked[None, :]).astype(jnp.int32), axis=1) - 1
 
 
 def on_device(

time: 562 us -> 563 us (level)
  no operation moved by 1% of the time
where the time goes in v1:
time: 563 us; the launch traced here: 555 us
  waiting for transfers between devices  417 us (74%)
  matrix products  50.6 us (9%)
  local copies, waits for them, and re-layouts  39 us (7%)
  other arithmetic  25.7 us (5%)
  between operations  14.9 us (3%)
  starting transfers between devices  7.91 us (1%)
    reduce_scatter x3, waiting for transfers between devices, on_device(): lax.psum_scatter(mixed_grad.astype(jnp.bfloat16), 'mp', scatter_dimension...  80.3 us
    all_gather x1, waiting for transfers between devices, on_device(): lax.all_gather(w_out[0], 'dp', axis=1, tiled=True)  76.6 us
    all_gather x1, waiting for transfers between devices, on_device(): lax.all_gather(w_query[0], 'dp', axis=1, tiled=True)  75.3 us
    all_gather x1, waiting for transfers between devices, on_device(): lax.all_gather(w_key[0], 'dp', axis=1, tiled=True)  66.5 us
    all_gather x2, waiting for transfers between devices, on_device(): full_section = lax.all_gather(own_section, 'mp', axis=1, tiled=True)  41.3 us
    all_gather x1, waiting for transfers between devices, on_device(): lax.all_gather(w_value[0], 'dp', axis=1, tiled=True)  35.9 us
    reduce_scatter x1, waiting for transfers between devices, on_device(): lax.psum_scatter(encoder_partial.astype(jnp.bfloat16), ('segment', 'mp'),...  34.4 us
    another operation x11, local copies, waits for them, and re-layouts  15.5 us
  transfers between devices with their start and end apart: 14, of which 11 were waited for; matrix products, arithmetic and copies ran while one was open for 10% of the time, Pallas kernels for 0%

profile of v1, /device:TPU:0, one launch (start us, length us, event | category | flops | bytes accessed | tf_op | source)
XLA Modules:
  0.0 555.4 jit_solution(12145603044757109902)
XLA Ops:
  8.8 2.4 dynamic-slice_select_fusion.2
  11.2 76.6 %all-gather.15.cloned.1.call-done = bf16[1,1024,2048]{2,1,0:T(8,128)(2,1)} async-done(((bf16[1,1024,256]{2,1,0:T(8,128)(2,1)}), bf16[1,1024,2048]{2,1,0:T(8,128)(2,1)}) %all-gather.15.cloned.1.call-update) | async-done | bytes 4194320 | tf_op jit(solution)/shard_map/all_gather | solution.py:124
  87.8 75.3 %all-gather.17.cloned.1.call-done = bf16[1,1024,2048]{2,1,0:T(8,128)(2,1)} async-done(((bf16[1,1024,256]{2,1,0:T(8,128)(2,1)}), bf16[1,1024,2048]{2,1,0:T(8,128)(2,1)}) %all-gather.17.cloned.1.call-update) | async-done | bytes 4194320 | tf_op jit(solution)/shard_map/all_gather | solution.py:125
  163.1 3.0 conditional.3
  166.3 46.4 %reduce-scatter.5.cloned.1.call-done = bf16[256,1024]{1,0:T(8,128)(2,1)} async-done(((bf16[256,2048]{1,0:T(8,128)(2,1)}), bf16[256,1024]{1,0:T(8,128)(2,1)}) %reduce-scatter.5.cloned.1.call-update) | async-done | bytes 524304 | tf_op jit(solution)/shard_map/reduce_scatter | solution.py:162
  213.8 2.4 select_dynamic-update-slice_fusion.7
  216.3 21.4 %all-gather.11.cloned.1.call-done = bf16[256,2048]{1,0:T(8,128)(2,1)} async-done(((bf16[256,1024]{1,0:T(8,128)(2,1)}), bf16[256,2048]{1,0:T(8,128)(2,1)}) %all-gather.11.cloned.1.call-update) | async-done | bytes 1048592 | tf_op jit(solution)/shard_map/all_gather | solution.py:170
  237.7 1.5 collective-permute-start
  239.2 3.4 collective-permute-done
  242.6 2.9 dynamic-slice_select_fusion.1
  245.5 31.3 %conditional.4 = (bf16[256,2048]{1,0:T(8,128)(2,1)}, bf16[384,1024]{0,1:T(8,128)(2,1)}, bf16[384,1024]{0,1:T(8,128)(2,1)}) conditional(s32[]{:T(128)} %convert_element_type.206, () %tuple.46, (s32[2,2]{1,0:T(2,128)S(1)}, s32[]{:T(128)}, s32[2,2]{1,0:T(2,128)S(1)}, s32[2,2]{1,0:T(2,128)S(1)}, bf16[1,512,1024]{2,1,0:T(8,128)(2,1)}, ...), branch_computations={%region_7.8_spmd, %region_8.13_spmd} | conditional | flops 3363606528 | bytes 75467568 | solution.py:156
  245.9 1.6 copy.92
  247.4 1.6 copy.93
  249.1 3.5 constant_dynamic-slice_fusion.6
  252.5 2.3 copy.91
  254.8 2.2 constant_dynamic-slice_fusion.8
  257.0 3.4 fusion.94
  260.4 4.6 convolution_convert_fusion.3
  265.0 2.0 copy.115
  267.1 2.5 fusion.21
  273.1 2.3 fusion.98
  275.4 1.4 convolution_convert_fusion.2
  276.9 20.4 %reduce-scatter.7.cloned.1.call-done = bf16[256,1024]{1,0:T(8,128)(2,1)} async-done(((bf16[256,2048]{1,0:T(8,128)(2,1)}), bf16[256,1024]{1,0:T(8,128)(2,1)}) %reduce-scatter.7.cloned.1.call-update) | async-done | bytes 524304 | tf_op jit(solution)/shard_map/reduce_scatter | solution.py:162
  297.3 2.7 select_dynamic-update-slice_fusion.6
  301.5 19.9 %all-gather.13.cloned.1.call-done = bf16[256,2048]{1,0:T(8,128)(2,1)} async-done(((bf16[256,1024]{1,0:T(8,128)(2,1)}), bf16[256,2048]{1,0:T(8,128)(2,1)}) %all-gather.13.cloned.1.call-update) | async-done | bytes 1048592 | tf_op jit(solution)/shard_map/all_gather | solution.py:170
  327.3 2.5 select_dynamic-update-slice_fusion.1
  329.8 2.7 select_dynamic-update-slice_fusion.4
  332.5 1.4 dynamic-slice_select_fusion
  333.9 25.3 %conditional.5 = (bf16[256,2048]{1,0:T(8,128)(2,1)S(1)}, bf16[384,1024]{0,1:T(8,128)(2,1)S(1)}, bf16[384,1024]{0,1:T(8,128)(2,1)S(1)}) conditional(s32[]{:T(128)} %convert_element_type.211, () %tuple.48, (s32[2,2]{1,0:T(2,128)S(1)}, s32[]{:T(128)}, s32[2,2]{1,0:T(2,128)S(1)}, s32[2,2]{1,0:T(2,128)S(1)}, bf16[1,512,1024]{2,1,0:T(8,128)(2,1)}, ...), branch_computations={%region_14.15_spmd, %region_15.20_spmd} | conditional | flops 3363606528 | bytes 90147712 | solution.py:156
  334.4 1.6 copy.95
  336.0 1.6 copy.96
  337.6 3.1 constant_dynamic-slice_fusion.12
  343.4 2.1 fusion.95
  345.5 4.4 convolution_convert_fusion.5
  351.1 2.2 fusion.38
  353.4 1.6 multiply_convert_fusion.5
  359.2 3.4 select_dynamic-update-slice_fusion
  362.6 35.9 %all-gather.21.cloned.1.call-done = bf16[1,1024,2048]{2,1,0:T(8,128)(2,1)} async-done(((bf16[1,1024,256]{2,1,0:T(8,128)(2,1)}), bf16[1,1024,2048]{2,1,0:T(8,128)(2,1)}) %all-gather.21.cloned.1.call-update) | async-done | bytes 4194320 | tf_op jit(solution)/shard_map/all_gather | solution.py:127
  398.5 8.8 %fusion.51 = f32[768,2048]{1,0:T(8,128)} fusion(bf16[768,1024]{0,1:T(8,128)(2,1)} %get-tuple-element.471, bf16[1,1024,2048]{2,1,0:T(8,128)(2,1)} %all-gather.21.cloned.1.call-done), kind=kOutput, calls=%fused_computation.106 | convolution fusion | flops 3221225472 | bytes 12058624 | tf_op jit(solution)/shard_map/dot_general | solution.py:188
  407.3 66.5 %all-gather.19.cloned.1.call-done = bf16[1,1024,2048]{2,1,0:T(8,128)(2,1)} async-done(((bf16[1,1024,256]{2,1,0:T(8,128)(2,1)}), bf16[1,1024,2048]{2,1,0:T(8,128)(2,1)}) %all-gather.19.cloned.1.call-update) | async-done | bytes 4194320 | tf_op jit(solution)/shard_map/all_gather | solution.py:126
  473.8 9.6 %add_convert_fusion = bf16[768,2048]{1,0:T(8,128)(2,1)} fusion(f32[768,2048]{1,0:T(8,128)} %fusion.51, bf16[768,1024]{0,1:T(8,128)(2,1)} %get-tuple-element.472, bf16[1,1024,2048]{2,1,0:T(8,128)(2,1)} %all-gather.19.cloned.1.call-done), kind=kOutput, calls=%fused_computation.105 | convolution fusion | flops 3224371200 | bytes 15204352 | tf_op jit(solution)/shard_map/dot_general | solution.py:188
  485.4 34.4 %reduce-scatter.11.cloned.1.call-done = bf16[768,512]{1,0:T(8,128)(2,1)} async-done(((bf16[768,2048]{1,0:T(8,128)(2,1)}), bf16[768,512]{1,0:T(8,128)(2,1)}) %reduce-scatter.11.cloned.1.call-update) | async-done | bytes 786448 | tf_op jit(solution)/shard_map/reduce_scatter | solution.py:191
  519.8 1.7 convolution_convert_fusion.6
  521.9 1.5 collective-permute-start.2
  524.2 3.3 collective-permute-start.3
  527.5 1.4 copy.139
  528.9 13.4 %reduce-scatter.9.cloned.1.call-done = bf16[256,1024]{1,0:T(8,128)(2,1)} async-done(((bf16[256,2048]{1,0:T(8,128)(2,1)}), bf16[256,1024]{1,0:T(8,128)(2,1)}) %reduce-scatter.9.cloned.1.call-update) | async-done | bytes 524304 | tf_op jit(solution)/shard_map/reduce_scatter | solution.py:162
  542.3 1.5 fusion.68
  (137 shorter events, 32.5 us)
Async XLA Ops:
  7.2 156.0 %copy-start = (bf16[1,768,1024]{2,1,0:T(8,128)(2,1)S(1)}, bf16[1,768,1024]{2,1,0:T(8,128)(2,1)}, u32[]{:S(2)}) copy-start(bf16[1,768,1024]{2,1,0:T(8,128)(2,1)} %param.20) | copy-start | bytes 4718596
  7.2 156.0 %copy-start.1 = (bf16[1,768,1024]{2,1,0:T(8,128)(2,1)S(1)}, bf16[1,768,1024]{2,1,0:T(8,128)(2,1)}, u32[]{:S(2)}) copy-start(bf16[1,768,1024]{2,1,0:T(8,128)(2,1)} %param.21) | copy-start | bytes 4718596
  7.2 155.9 %copy-start.22 = (s32[2,2]{1,0:T(2,128)S(1)}, s32[2,2]{1,0:T(2,128)}, u32[]{:S(2)}) copy-start(s32[2,2]{1,0:T(2,128)} %param.26) | copy-start | bytes 52
  7.2 155.9 %copy-start.23 = (s32[2,2]{1,0:T(2,128)S(1)}, s32[2,2]{1,0:T(2,128)}, u32[]{:S(2)}) copy-start(s32[2,2]{1,0:T(2,128)} %param.27) | copy-start | bytes 52
  7.2 155.9 %copy-start.24 = (s32[2,2]{1,0:T(2,128)S(1)}, s32[2,2]{1,0:T(2,128)}, u32[]{:S(2)}) copy-start(s32[2,2]{1,0:T(2,128)} %param.28) | copy-start | bytes 52
  7.2 80.6 %all-gather.15.cloned.1.call-start = ((), (), s32[]{:S(2)}) async-start(), calls=%async_computation.10 | async-start | bytes 4718592 | tf_op jit(solution)/shard_map/all_gather | solution.py:124
  7.9 155.2 %all-gather.17.cloned.1.call-start = ((), (), s32[]{:S(2)}) async-start(), calls=%async_computation.11 | async-start | bytes 4718592 | tf_op jit(solution)/shard_map/all_gather | solution.py:125
  8.7 204.0 %reduce-scatter.5.cloned.1.call-start = ((), (), s32[]{:S(2)}) async-start(), calls=%async_computation.4 | async-start | bytes 1572864 | tf_op jit(solution)/shard_map/reduce_scatter | solution.py:162
  166.2 71.5 %all-gather.11.cloned.1.call-start = ((), (), s32[]{:S(2)}) async-start(), calls=%async_computation.5 | async-start | bytes 1572864 | tf_op jit(solution)/shard_map/all_gather | solution.py:170
  216.2 81.1 %reduce-scatter.7.cloned.1.call-start = ((), (), s32[]{:S(2)}) async-start(), calls=%async_computation.6 | async-start | bytes 1572864 | tf_op jit(solution)/shard_map/reduce_scatter | solution.py:162
  237.7 4.9 collective-permute-start
  267.1 2.5 copy-start.16
  267.1 2.5 copy-start.19
  267.1 2.7 copy-start.30
  269.7 1.0 copy-start.13
  269.7 3.3 copy-start.27
  270.8 1.8 copy-start.8
  276.8 44.6 %all-gather.13.cloned.1.call-start = ((), (), s32[]{:S(2)}) async-start(), calls=%async_computation.7 | async-start | bytes 1572864 | tf_op jit(solution)/shard_map/all_gather | solution.py:170
  300.0 98.6 %all-gather.21.cloned.1.call-start = ((), (), s32[]{:S(2)}) async-start(), calls=%async_computation.13 | async-start | bytes 4718592 | tf_op jit(solution)/shard_map/all_gather | solution.py:127
  300.7 173.1 %all-gather.19.cloned.1.call-start = ((), (), s32[]{:S(2)}) async-start(), calls=%async_computation.12 | async-start | bytes 4718592 | tf_op jit(solution)/shard_map/all_gather | solution.py:126
  301.5 218.3 %reduce-scatter.11.cloned.1.call-start = ((), (), s32[]{:S(2)}) async-start(), calls=%async_computation.9 | async-start | bytes 3932160 | tf_op jit(solution)/shard_map/reduce_scatter | solution.py:191
  321.4 11.1 %collective-permute-start.1 = (bf16[256,2048]{1,0:T(8,128)(2,1)}, bf16[256,2048]{1,0:T(8,128)(2,1)S(1)}, u32[]{:S(2)}, u32[]{:S(2)}) collective-permute-start(bf16[256,2048]{1,0:T(8,128)(2,1)} %all-gather.13.cloned.1.call-done), channel_id=1, source_target_pairs={{16,0},{17,1},{18,2},{19,3},{20,4},{21,5},{22,6},{23,7},{24,8},{25... | collective-permute-start | bytes 3145736 | tf_op jit(solution)/shard_map/ppermute | solution.py:17
  329.8 2.7 copy-start.3
  336.0 1.6 copy-start.6
  337.6 3.1 copy-start.2
  340.8 2.6 copy-start.9
  343.4 2.1 copy-start.11
  345.5 5.6 %copy-start.17 = (bf16[1,384,1024]{1,2,0:T(8,128)(2,1)S(1)}, bf16[1,384,1024]{1,2,0:T(8,128)(2,1)}, u32[]{:S(2)}) copy-start(bf16[1,384,1024]{1,2,0:T(8,128)(2,1)} %get-tuple-element.457) | copy-start | bytes 2359300 | tf_op jit(solution)/shard_map/cond
  351.1 2.2 copy-start.20
  351.1 2.2 copy-start.31
  355.0 2.2 copy-start.28
  357.2 1.3 copy-start.21
  359.2 3.4 copy-start.5
  483.5 0.7 copy-start.25
  483.5 58.9 %reduce-scatter.9.cloned.1.call-start = ((), (), s32[]{:S(2)}) async-start(), calls=%async_computation.8 | async-start | bytes 1572864 | tf_op jit(solution)/shard_map/reduce_scatter | solution.py:162
  521.9 20.4 %copy-start.10 = (bf16[256,2048]{1,0:T(8,128)(2,1)S(1)}, bf16[256,2048]{1,0:T(8,128)(2,1)}, u32[]{:S(2)}) copy-start(bf16[256,2048]{1,0:T(8,128)(2,1)} %dynamic-slice_select_fusion) | copy-start | bytes 3145732
  521.9 22.3 %collective-permute-start.2 = (bf16[256,512]{1,0:T(8,128)(2,1)S(1)}, bf16[256,512]{1,0:T(8,128)(2,1)S(1)}, u32[]{:S(2)}, u32[]{:S(2)}) collective-permute-start(bf16[256,512]{1,0:T(8,128)(2,1)S(1)} %bitcast.229), channel_id=1, source_target_pairs={{0,2},{2,4},{4,6},{6,8},{8,10},{10,12},{12,14},{14,0},{1,3},{3,5},... | collective-permute-start | bytes 786440 | tf_op jit(solution)/shard_map/ppermute | solution.py:26
  524.2 20.4 %collective-permute-start.3 = (bf16[256,512]{1,0:T(8,128)(2,1)}, bf16[256,512]{1,0:T(8,128)(2,1)}, u32[]{:S(2)}, u32[]{:S(2)}) collective-permute-start(bf16[256,512]{1,0:T(8,128)(2,1)} %bitcast.62), channel_id=1, source_target_pairs={{2,0},{4,2},{6,4},{8,6},{10,8},{12,10},{14,12},{0,14},{3,1},{5,3},... | collective-permute-start | bytes 786440 | tf_op jit(solution)/shard_map/ppermute | solution.py:29
  528.9 14.9 %copy-start.4 = (bf16[768,512]{1,0:T(8,128)(2,1)S(1)}, bf16[768,512]{1,0:T(8,128)(2,1)}, u32[]{:S(2)}) copy-start(bf16[768,512]{1,0:T(8,128)(2,1)} %reduce-scatter.11.cloned.1.call-done) | copy-start | bytes 2359300
  543.8 1.0 copy-start.14
Sparse Core Ops, SparseCore 0:
  10.1 77.7 all-gather.14
  89.9 73.1 all-gather.16
  166.3 46.3 reduce-scatter.4
  216.3 21.3 all-gather.10
  276.9 20.3 reduce-scatter.6
  300.1 21.3 all-gather.12
  323.5 75.0 all-gather.20
  400.6 73.1 all-gather.18
  483.6 36.1 reduce-scatter.10
  522.0 20.3 reduce-scatter.8

commit v2 on v1

v2 whole, which is shorter than its diff:
```python
import functools

import jax
import jax.numpy as jnp
from jax import lax
from jax.experimental import pallas as pl
from jax.experimental.pallas import tpu as pltpu
from jax.sharding import PartitionSpec as P

DH = 256
TILE = 128
CAP = 2
BLOCK = 256
masked_floor = -1e30
BF16, F32 = jnp.bfloat16, jnp.float32


def dot(a, b, ca, cb):
    return lax.dot_general(a, b, (((ca,), (cb,)), ((), ())), preferred_element_type=F32)


def tick_kernel(count, half, sc, g_ref, q_ref, k_ref, v_ref, *rest):
    wo, wq = rest[:count], rest[count : 2 * count]
    mixed_ref, kg_ref, vg_ref, acc = rest[2 * count :]
    head = pl.program_id(0)
    per = half // BLOCK
    scale = DH ** (-0.5)

    def place(b):
        src = sc[b]
        return src // per, pl.ds(pl.multiple_of((src % per) * BLOCK, BLOCK), BLOCK)

    og = None
    for b in range(count):
        at, cols = place(b)
        term = dot(g_ref[at, :, cols], wo[b][...], 1, 1)
        og = term if og is None else og + term
    og = og.astype(BF16)
    q, k, v = q_ref[0], k_ref[0], v_ref[0]
    scores = dot(q, k, 1, 1) * scale
    rows = lax.broadcasted_iota(jnp.int32, scores.shape, 0)
    cols_id = lax.broadcasted_iota(jnp.int32, scores.shape, 1)
    allowed = None
    for e in range(2):
        q_len, k_off, k_len = sc[count + e], sc[count + 2 + e] * TILE, sc[count + 4 + e]
        hit = (rows >= e * TILE) & (rows < e * TILE + q_len)
        hit = hit & (cols_id >= k_off) & (cols_id < k_off + k_len)
        allowed = hit if allowed is None else allowed | hit
    masked = jnp.where(allowed, scores, masked_floor)
    top = jnp.max(masked, axis=-1, keepdims=True)
    terms = jnp.where(allowed, jnp.exp(masked - top), 0.0)
    prob = terms / jnp.maximum(jnp.sum(terms, axis=-1, keepdims=True), 1.0)
    prob_bf = prob.astype(BF16)
    attended = dot(prob_bf, v, 1, 0)
    out_dot = jnp.sum(og.astype(F32) * attended, axis=-1, keepdims=True)
    sg = (prob * (dot(og, v, 1, 1) - out_dot)).astype(BF16)
    qg = (dot(sg, k, 1, 0) * scale).astype(BF16)
    kg_ref[...] = (dot(sg, q, 0, 0) * scale).astype(BF16)
    vg_ref[...] = dot(prob_bf, og, 0, 0).astype(BF16)

    @pl.when(head == 0)
    def _():
        acc[...] = jnp.zeros_like(acc)

    for b in range(count):
        at, cols = place(b)
        acc[at, :, cols] += dot(qg, wq[b][...], 1, 0)

    @pl.when(head == pl.num_programs(0) - 1)
    def _():
        mixed_ref[...] = acc[...].astype(BF16)


def run_tick(scalars, grad, at, seq, saved_q, saved_k, saved_v, wo, wq, q_rows, k_rows):
    half = grad.shape[2]
    heads = saved_q.shape[2] // DH
    count = len(wo)
    weight = pl.BlockSpec((DH, BLOCK), lambda h, sc: (h, 0))
    macs = heads * q_rows * DH * (4 * half + 6 * k_rows)
    return pl.pallas_call(
        functools.partial(tick_kernel, count, half),
        grid_spec=pltpu.PrefetchScalarGridSpec(
            num_scalar_prefetch=1,
            grid=(heads,),
            in_specs=[
                pl.BlockSpec((2, q_rows, half), lambda h, sc: (0, at, 0)),
                pl.BlockSpec((1, q_rows, DH), lambda h, sc: (0, seq, h)),
                pl.BlockSpec((1, k_rows, DH), lambda h, sc: (0, seq, h)),
                pl.BlockSpec((1, k_rows, DH), lambda h, sc: (0, seq, h)),
            ]
            + [weight] * (2 * count),
            out_specs=[
                pl.BlockSpec((2, q_rows, half), lambda h, sc: (0, 0, 0)),
                pl.BlockSpec((k_rows, DH), lambda h, sc: (0, h)),
                pl.BlockSpec((k_rows, DH), lambda h, sc: (0, h)),
            ],
            scratch_shapes=[pltpu.VMEM((2, q_rows, half), F32)],
        ),
        out_shape=[
            jax.ShapeDtypeStruct((2, q_rows, half), BF16),
            jax.ShapeDtypeStruct((k_rows, heads * DH), BF16),
            jax.ShapeDtypeStruct((k_rows, heads * DH), BF16),
        ],
        compiler_params=pltpu.CompilerParams(vmem_limit_bytes=40 << 20),
        cost_estimate=pl.CostEstimate(
            flops=2 * macs, bytes_accessed=16 << 20, transcendentals=heads * q_rows * k_rows
        ),
    )(scalars, grad, saved_q, saved_k, saved_v, *wo, *wq)


def encoder_kernel(count, quarter, sc, kg_ref, vg_ref, *rest):
    wk, wv, out_ref = rest[:count], rest[count : 2 * count], rest[2 * count]
    per = quarter // BLOCK
    kg, vg = kg_ref[...], vg_ref[...]
    for b in range(count):
        src = sc[b]
        cols = pl.ds(pl.multiple_of((src % per) * BLOCK, BLOCK), BLOCK)
        part = dot(kg, wk[b][...], 1, 0) + dot(vg, wv[b][...], 1, 0)
        out_ref[src // per, :, cols] = part.astype(BF16)


def run_encoder(scalars, kg, vg, wk, wv):
    count = len(wk)
    rows, depth = kg.shape
    quarter = count * BLOCK // 4
    step = 256
    whole = pl.BlockSpec((depth, BLOCK), lambda i, sc: (0, 0))
    return pl.pallas_call(
        functools.partial(encoder_kernel, count, quarter),
        grid_spec=pltpu.PrefetchScalarGridSpec(
            num_scalar_prefetch=1,
            grid=(rows // step,),
            in_specs=[pl.BlockSpec((step, depth), lambda i, sc: (i, 0))] * 2
            + [whole] * (2 * count),
            out_specs=pl.BlockSpec((4, step, quarter), lambda i, sc: (0, i, 0)),
        ),
        out_shape=jax.ShapeDtypeStruct((4, rows, quarter), BF16),
        compiler_params=pltpu.CompilerParams(vmem_limit_bytes=48 << 20),
        cost_estimate=pl.CostEstimate(
            flops=16 * rows * depth * quarter, bytes_accessed=14 << 20, transcendentals=0
        ),
    )(scalars, kg, vg, *wk, *wv)


def pick_kernel(sc, own_ref, other_ref, local_ref, left_ref, right_ref):
    local_ref[...] = (own_ref[...].astype(F32) + other_ref[...].astype(F32)).astype(BF16)
    for c in range(CAP):
        left_ref[c] = local_ref[sc[c]]
        right_ref[c] = local_ref[sc[CAP + c]]


def place_kernel(sc, left_ref, local_ref, right_ref, out_ref):
    tiles = local_ref.shape[0]
    for s in range(tiles):
        i = sc[s]

        @pl.when(i < CAP)
        def _():
            out_ref[s] = left_ref[jnp.minimum(i, CAP - 1)]

        @pl.when((i >= CAP) & (i < CAP + tiles))
        def _():
            out_ref[s] = local_ref[jnp.clip(i - CAP, 0, tiles - 1)]

        @pl.when(i >= CAP + tiles)
        def _():
            out_ref[s] = right_ref[jnp.clip(i - CAP - tiles, 0, CAP - 1)]


def small_call(body, scalars, arrays, outs):
    vmem = pl.BlockSpec(memory_space=pltpu.VMEM)
    single = not isinstance(outs, list)
    return pl.pallas_call(
        body,
        in_specs=[pl.BlockSpec(memory_space=pltpu.SMEM)] + [vmem] * len(arrays),
        out_specs=vmem if single else [vmem] * len(outs),
        out_shape=outs,
        compiler_params=pltpu.CompilerParams(vmem_limit_bytes=24 << 20),
    )(scalars, *arrays)


def gathered(shard, factors):
    count = lax.axis_size("dp")
    me = lax.axis_index("dp")
    if shard.shape[1] != BLOCK or factors is None:
        full = lax.all_gather(shard, "dp", axis=1, tiled=True)
        blocks = [full[:, i : i + BLOCK] for i in range(0, full.shape[1], BLOCK)]
        return blocks, list(jnp.arange(len(blocks), dtype=jnp.int32))
    outer, inner = factors
    ring = [(i, (i + inner) % count) for i in range(count)]
    swap = [(i, i ^ 1) for i in range(count)]
    blocks, sources = [], []
    block = shard
    for r in range(outer):
        if r:
            block = lax.ppermute(block, "dp", ring)
        source = (me - r * inner + count) % count
        blocks.append(block)
        sources.append(source)
        blocks.append(lax.ppermute(block, "dp", swap))
        sources.append(source ^ 1)
    return blocks, sources


def ranked(marked):
    ids = jnp.arange(marked.shape[0], dtype=jnp.int32)
    upto = ids[None, :] <= ids[:, None]
    return jnp.sum((upto & marked[None, :]).astype(jnp.int32), axis=1) - 1


def on_device(
    grad_top,
    saved_query,
    saved_key,
    saved_value,
    w_query,
    w_key,
    w_value,
    w_out,
    query_length,
    key_offset,
    key_length,
    tile_owner,
):
    seg = lax.axis_index("segment")
    mp = lax.axis_index("mp")
    devices = lax.axis_size("dp")
    me = lax.axis_index("dp")
    micro = query_length.shape[0]
    q_rows = grad_top.shape[0] // micro
    k_rows = saved_key.shape[1] // micro
    half = grad_top.shape[1] // 2
    factors = (devices // 2, 2) if devices % 2 == 0 else None
    wo, sources = gathered(w_out[0], factors)
    wq, _ = gathered(w_query[0], factors)
    wk, _ = gathered(w_key[0], factors)
    wv, _ = gathered(w_value[0], factors)
    order = jnp.stack(sources).astype(jnp.int32)

    mp_swap = [(0, 1), (1, 0)]
    top = grad_top.reshape(grad_top.shape[0], 2, half).transpose(1, 0, 2)
    scalars = [
        jnp.concatenate([order, query_length[s], key_offset[s], key_length[s]])
        for s in range(micro)
    ]

    def tick(s, grad, at):
        return run_tick(
            scalars[s], grad, at, s, saved_query, saved_key, saved_value, wo, wq, q_rows, k_rows
        )

    upper = [tick(s, top, s) for s in range(micro)]
    upper_half, incoming = [], []
    for s in range(micro):
        mixed = upper[s][0]
        other = lax.ppermute(mixed, "mp", mp_swap)
        rows = top[:, s * q_rows : (s + 1) * q_rows]
        section = (rows.astype(F32) + (mixed.astype(F32) + other.astype(F32))).astype(BF16)
        incoming.append(lax.ppermute(section, "segment", [(1, 0)]))
        upper_half.append(lax.dynamic_index_in_dim(section, mp, 0, keepdims=False))
    lower = [tick(s, incoming[s], 0) for s in range(micro)]
    halves = []
    for s in range(micro):
        mixed = lower[s][0]
        other = lax.ppermute(
            lax.dynamic_index_in_dim(mixed, 1 - mp, 0, keepdims=False), "mp", mp_swap
        )
        own = lax.dynamic_index_in_dim(mixed, mp, 0, keepdims=False)
        base = lax.dynamic_index_in_dim(incoming[s], mp, 0, keepdims=False)
        low = (base.astype(F32) + (own.astype(F32) + other.astype(F32))).astype(BF16)
        halves.append(jnp.where(seg == 1, upper_half[s], low))
    sections = jnp.concatenate(halves, axis=0)

    kg = jnp.concatenate([jnp.where(seg == 1, upper[s][1], lower[s][1]) for s in range(micro)], 0)
    vg = jnp.concatenate([jnp.where(seg == 1, upper[s][2], lower[s][2]) for s in range(micro)], 0)
    parts = run_encoder(order, kg, vg, wk, wv)
    away = lax.dynamic_slice_in_dim(parts, (1 - seg) * 2, 2, 0)
    mine = lax.dynamic_slice_in_dim(parts, seg * 2, 2, 0)
    arrived = lax.ppermute(away, "segment", mp_swap)
    summed = (mine.astype(F32) + arrived.astype(F32)).astype(BF16)
    crossing = lax.ppermute(
        lax.dynamic_index_in_dim(summed, 1 - mp, 0, keepdims=False), "mp", mp_swap
    )
    kept = lax.dynamic_index_in_dim(summed, mp, 0, keepdims=False)

    tiles = kept.shape[0] // TILE
    features = kept.shape[1]
    owners = tile_owner.reshape(devices, tiles)
    slot_ids = jnp.arange(CAP, dtype=jnp.int32)[:, None]
    tile_ids = jnp.arange(tiles, dtype=jnp.int32)

    def plan(source):
        source = source % devices
        row = lax.dynamic_index_in_dim(owners, source, 0, keepdims=False)
        return (row // tiles - source + devices) % devices, row % tiles

    def ranks_of(marked):
        return (ranked(marked)[None, :] == slot_ids) & marked[None, :]

    step, slot = plan(me)
    left_step, left_slot = plan(me - 1 + devices)
    right_step, right_slot = plan(me + 1)
    send_left = jnp.sum(jnp.where(ranks_of(step == devices - 1), tile_ids[None, :], 0), axis=1)
    send_right = jnp.sum(jnp.where(ranks_of(step == 1), tile_ids[None, :], 0), axis=1)
    left_hit = ranks_of(left_step == 1)
    right_hit = ranks_of(right_step == devices - 1)
    target = jnp.concatenate(
        [
            jnp.sum(jnp.where(left_hit, left_slot[None, :], 0), axis=1),
            slot,
            jnp.sum(jnp.where(right_hit, right_slot[None, :], 0), axis=1),
        ]
    )
    usable = jnp.concatenate([jnp.any(left_hit, axis=1), step == 0, jnp.any(right_hit, axis=1)])
    chosen = (tile_ids[:, None] == target[None, :]) & usable[None, :]
    candidate_ids = jnp.arange(target.shape[0], dtype=jnp.int32)
    take = jnp.sum(jnp.where(chosen, candidate_ids[None, :], 0), axis=1)

    tiled = (tiles, TILE, features)
    shape = jax.ShapeDtypeStruct(tiled, BF16)
    handed = jax.ShapeDtypeStruct((CAP, TILE, features), BF16)
    local, to_left, to_right = small_call(
        pick_kernel,
        jnp.concatenate([send_left, send_right]),
        [kept.reshape(tiled), crossing.reshape(tiled)],
        [shape, handed, handed],
    )
    forward = [(i, (i + 1) % devices) for i in range(devices)]
    backward = [(b, a) for a, b in forward]
    from_left = lax.ppermute(to_right, "dp", forward)
    from_right = lax.ppermute(to_left, "dp", backward)
    owned = small_call(place_kernel, take, [from_left, local, from_right], shape)
    return sections[None], owned.reshape(tiles * TILE, features)


def solution(mesh):
    in_specs = (
        P("dp", None),
        P("segment", "dp", "mp"),
        P("segment", "dp", "mp"),
        P("segment", "dp", "mp"),
        P("segment", "mp", "dp"),
        P("segment", "mp", "dp"),
        P("segment", "mp", "dp"),
        P("segment", "mp", "dp"),
        P("dp", None),
        P("dp", None),
        P("dp", None),
        P(),
    )
    out_specs = (P("segment", "dp", "mp"), P("dp", ("segment", "mp")))
    return jax.shard_map(
        on_device, mesh=mesh, in_specs=in_specs, out_specs=out_specs, check_vma=False
    )
```

time: 563 us -> 377 us (0.67); the launches traced: 555 us -> 377 us
  waiting for transfers between devices: 417 us -> 244 us
  Pallas kernels: 0 us -> 55.4 us
  matrix products: 50.6 us -> 0 us
  starting transfers between devices: 7.91 us -> 40.4 us
  local copies, waits for them, and re-layouts: 39 us -> 23.7 us
  other arithmetic: 25.7 us -> 11.7 us
  between operations: 14.9 us -> 1.12 us
    all_gather x6 -> x0, waiting for transfers between devices: 296 us -> none  [the longest x1 76.6 us: on_device(): lax.all_gather(w_out[0], 'dp', axis=1, tiled=True)]
    ppermute x4 -> x38, waiting for transfers between devices: 3.43 us -> 244 us  [the longest x12 92.2 us: gathered(): block = lax.ppermute(block, 'dp', ring)]
    reduce_scatter x4 -> x0, waiting for transfers between devices: 115 us -> none  [the longest x3 80.3 us: on_device(): lax.psum_scatter(mixed_grad.astype(jnp.bfloat16), 'mp', scatter_dimension...]
    pallas_call x0 -> x7, Pallas kernels: none -> 55.4 us  [the longest x4 41.4 us: run_tick(): pl.pallas_call(functools.partial(tick_kernel, count, half), grid_spec=plt...]
    dot_general x18 -> x0, matrix products: 45.2 us -> none  [the longest x1 9.65 us: on_device(): jnp.dot(key_grads, key_full, preferred_element_type=jnp.float32)]
    ppermute x4 -> x38, starting transfers between devices: 7.51 us -> 40.4 us  [the longest x16 19.7 us: gathered(): blocks.append(lax.ppermute(block, 'dp', swap))]
    select_n x12 -> x7, other arithmetic: 24 us -> 3.33 us  [the longest x2 2.97 us: on_device(): halves.append(jnp.where(seg == 1, upper_half[s], low))]
    another operation x11 -> x1, local copies, waits for them, and re-layouts: 15.5 us -> 0.09 us  [on_device(): order = jnp.stack(sources).astype(jnp.int32)]
  transfers between devices with their start and end apart: 14 -> 38, of which waited for: 11 -> 28; matrix products, arithmetic and copies ran while one was open for 10% -> 5% of each run, Pallas kernels for 0% -> 8%
where the time goes in v2:
time: 377 us
  waiting for transfers between devices  244 us (65%)
  Pallas kernels  55.4 us (15%)
  starting transfers between devices  40.4 us (11%)
  local copies, waits for them, and re-layouts  23.7 us (6%)
  other arithmetic  11.7 us (3%)
    ppermute x12, waiting for transfers between devices, gathered(): block = lax.ppermute(block, 'dp', ring)  92.2 us
    ppermute x16, waiting for transfers between devices, gathered(): blocks.append(lax.ppermute(block, 'dp', swap))  87.4 us
    pallas_call x4, Pallas kernels, run_tick(): pl.pallas_call(functools.partial(tick_kernel, count, half), grid_spec=plt...  41.4 us
    ppermute x2, waiting for transfers between devices, on_device(): other = lax.ppermute(mixed, 'mp', mp_swap)  32.5 us
    ppermute x16, starting transfers between devices, gathered(): blocks.append(lax.ppermute(block, 'dp', swap))  19.7 us
    unnamed x88, local copies, waits for them, and re-layouts  17.4 us
    ppermute x1, waiting for transfers between devices, on_device(): lax.ppermute(lax.dynamic_index_in_dim(summed, 1 - mp, 0, keepdims=False),...  15.3 us
    ppermute x2, waiting for transfers between devices, on_device(): lax.ppermute(lax.dynamic_index_in_dim(mixed, 1 - mp, 0, keepdims=False),...  14 us
  transfers between devices with their start and end apart: 38, of which 28 were waited for; matrix products, arithmetic and copies ran while one was open for 5% of the time, Pallas kernels for 8%

profile of v2, /device:TPU:0, one launch (start us, length us, event | category | flops | bytes accessed | tf_op | source)
XLA Modules:
  0.0 376.7 jit_solution(9979249001367039072)
XLA Ops:
  0.6 3.1 collective-permute-start.1
  3.7 1.6 collective-permute-start.8
  5.3 13.4 %collective-permute-done.1.rest_2_ = bf16[1024,256]{1,0:T(8,128)(2,1)S(1)} collective-permute-done((bf16[1024,256]{1,0:T(8,128)(2,1)}, bf16[1024,256]{1,0:T(8,128)(2,1)S(1)}, u32[]{:S(2)}, u32[]{:S(2)}) %collective-permute-start.1) | collective-permute-done | bytes 524320 | tf_op jit(solution)/shard_map/ppermute | solution.py:196
  18.7 11.3 %collective-permute-done.8.rest_10_ = bf16[1024,256]{1,0:T(8,128)(2,1)} collective-permute-done((bf16[1024,256]{1,0:T(8,128)(2,1)}, bf16[1024,256]{1,0:T(8,128)(2,1)}, u32[]{:S(2)}, u32[]{:S(2)}) %collective-permute-start.8) | collective-permute-done | bytes 524320 | tf_op jit(solution)/shard_map/ppermute | solution.py:196
  30.1 1.7 collective-permute-start
  32.1 1.7 collective-permute-start.2
  34.6 6.7 %collective-permute-done.3.rest_4_ = bf16[1024,256]{1,0:T(8,128)(2,1)} collective-permute-done((bf16[1024,256]{1,0:T(8,128)(2,1)S(1)}, bf16[1024,256]{1,0:T(8,128)(2,1)}, u32[]{:S(2)}, u32[]{:S(2)}) %collective-permute-start.3) | collective-permute-done | bytes 524320 | tf_op jit(solution)/shard_map/ppermute | solution.py:196
  41.3 11.2 %collective-permute-done.10.rest_12_ = bf16[1024,256]{1,0:T(8,128)(2,1)} collective-permute-done((bf16[1024,256]{1,0:T(8,128)(2,1)}, bf16[1024,256]{1,0:T(8,128)(2,1)}, u32[]{:S(2)}, u32[]{:S(2)}) %collective-permute-start.10) | collective-permute-done | bytes 524320 | tf_op jit(solution)/shard_map/ppermute | solution.py:196
  53.3 1.7 collective-permute-start.9
  57.2 1.7 collective-permute-start.4
  58.9 8.7 %collective-permute-done.2.rest_3_ = bf16[1024,256]{1,0:T(8,128)(2,1)S(1)} collective-permute-done((bf16[1024,256]{1,0:T(8,128)(2,1)S(1)}, bf16[1024,256]{1,0:T(8,128)(2,1)S(1)}, u32[]{:S(2)}, u32[]{:S(2)}) %collective-permute-start.2) | collective-permute-done | bytes 524320 | tf_op jit(solution)/shard_map/ppermute | solution.py:200
  68.4 1.7 collective-permute-start.11
  70.5 3.7 collective-permute-done.12.rest_14_
  74.1 1.5 collective-permute-start.13
  75.6 4.0 %copy.18 = bf16[512,2048]{0,1:T(8,128)(2,1)} copy(bf16[512,2048]{1,0:T(8,128)(2,1)} %param.12) | data formatting | bytes 4194304 | tf_op args[0]
  79.7 4.1 %copy.19 = bf16[512,2,1024]{2,0,1:T(8,128)(2,1)} copy(bf16[512,2,1024]{0,2,1:T(8,128)(2,1)} %bitcast.97) | data formatting | bytes 4194304 | tf_op jit(solution)/shard_map/reshape | solution.py:241
  84.0 6.2 %collective-permute-done.4.rest_5_ = bf16[1024,256]{1,0:T(8,128)(2,1)} collective-permute-done((bf16[1024,256]{1,0:T(8,128)(2,1)}, bf16[1024,256]{1,0:T(8,128)(2,1)}, u32[]{:S(2)}, u32[]{:S(2)}) %collective-permute-start.4) | collective-permute-done | bytes 524320 | tf_op jit(solution)/shard_map/ppermute | solution.py:200
  90.2 11.2 %collective-permute-done.11.rest_13_ = bf16[1024,256]{1,0:T(8,128)(2,1)} collective-permute-done((bf16[1024,256]{1,0:T(8,128)(2,1)}, bf16[1024,256]{1,0:T(8,128)(2,1)}, u32[]{:S(2)}, u32[]{:S(2)}) %collective-permute-start.11) | collective-permute-done | bytes 524320 | tf_op jit(solution)/shard_map/ppermute | solution.py:200
  101.4 11.2 %collective-permute-done.6.rest_7_ = bf16[1024,256]{1,0:T(8,128)(2,1)} collective-permute-done((bf16[1024,256]{1,0:T(8,128)(2,1)}, bf16[1024,256]{1,0:T(8,128)(2,1)}, u32[]{:S(2)}, u32[]{:S(2)}) %collective-permute-start.6) | collective-permute-done | bytes 524320 | tf_op jit(solution)/shard_map/ppermute | solution.py:200
  112.7 8.6 %collective-permute-done.13.rest_15_ = bf16[1024,256]{1,0:T(8,128)(2,1)} collective-permute-done((bf16[1024,256]{1,0:T(8,128)(2,1)}, bf16[1024,256]{1,0:T(8,128)(2,1)}, u32[]{:S(2)}, u32[]{:S(2)}) %collective-permute-start.13) | collective-permute-done | bytes 524320 | tf_op jit(solution)/shard_map/ppermute | solution.py:200
  126.5 10.4 %shard_map.131 = (bf16[2,256,1024]{2,1,0:T(8,128)(2,1)S(1)}, bf16[384,1024]{1,0:T(8,128)(2,1)S(1)}, bf16[384,1024]{1,0:T(8,128)(2,1)S(1)}) custom-call(s32[14]{0:T(128)S(1)} %concatenate.26.sc, bf16[2,512,1024]{2,1,0:T(8,128)(2,1)} %bitcast.94, bf16[1,512,1024]{2,1,0:T(8,128)(2,1)S(1)} %copy-done.1, bf16[1,768,1024]{2,1,0:T(8,128)(2,1)S(1)} %copy-done, ...), custom_call_target="tpu_custom_call" | custom-call | flops 3355443200 | bytes 16777216 | tf_op jit(solution)/shard_map/pallas_call | solution.py:80
  139.1 10.4 %shard_map.133 = (bf16[2,256,1024]{2,1,0:T(8,128)(2,1)S(1)}, bf16[384,1024]{1,0:T(8,128)(2,1)S(1)}, bf16[384,1024]{1,0:T(8,128)(2,1)S(1)}) custom-call(s32[14]{0:T(128)S(1)} %concatenate.27.sc, bf16[2,512,1024]{2,1,0:T(8,128)(2,1)} %bitcast.95, bf16[1,512,1024]{2,1,0:T(8,128)(2,1)S(1)} %copy-done.1, bf16[1,768,1024]{2,1,0:T(8,128)(2,1)S(1)} %copy-done, ...), custom_call_target="tpu_custom_call" | custom-call | flops 3355443200 | bytes 16777216 | tf_op jit(solution)/shard_map/pallas_call | solution.py:80
  150.3 13.6 %collective-permute-done.14 = bf16[2,256,1024]{2,1,0:T(8,128)(2,1)S(1)} collective-permute-done((bf16[2,256,1024]{2,1,0:T(8,128)(2,1)S(1)}, bf16[2,256,1024]{2,1,0:T(8,128)(2,1)S(1)}, u32[]{:S(2)}, u32[]{:S(2)}) %collective-permute-start.14) | collective-permute-done | bytes 1048608 | tf_op jit(solution)/shard_map/ppermute | solution.py:256
  163.9 18.9 %collective-permute-done.17 = bf16[2,256,1024]{2,1,0:T(8,128)(2,1)S(1)} collective-permute-done((bf16[2,256,1024]{2,1,0:T(8,128)(2,1)S(1)}, bf16[2,256,1024]{2,1,0:T(8,128)(2,1)S(1)}, u32[]{:S(2)}, u32[]{:S(2)}) %collective-permute-start.17) | collective-permute-done | bytes 1048608 | tf_op jit(solution)/shard_map/ppermute | solution.py:256
  182.8 2.9 add_convert_fusion.2
  188.3 1.6 collective-permute-start.28
  191.9 12.1 %collective-permute-done.21.rest_2_ = bf16[1024,256]{1,0:T(8,128)(2,1)} collective-permute-done((bf16[1024,256]{1,0:T(8,128)(2,1)}, bf16[1024,256]{1,0:T(8,128)(2,1)}, u32[]{:S(2)}, u32[]{:S(2)}) %collective-permute-start.21) | collective-permute-done | bytes 524320 | tf_op jit(solution)/shard_map/ppermute | solution.py:196
  205.2 10.0 %collective-permute-done.28.rest_10_ = bf16[1024,256]{1,0:T(8,128)(2,1)} collective-permute-done((bf16[1024,256]{1,0:T(8,128)(2,1)}, bf16[1024,256]{1,0:T(8,128)(2,1)}, u32[]{:S(2)}, u32[]{:S(2)}) %collective-permute-start.28) | collective-permute-done | bytes 524320 | tf_op jit(solution)/shard_map/ppermute | solution.py:196
  217.6 10.3 %shard_map.134 = (bf16[2,256,1024]{2,1,0:T(8,128)(2,1)S(1)}, bf16[384,1024]{1,0:T(8,128)(2,1)S(1)}, bf16[384,1024]{1,0:T(8,128)(2,1)S(1)}) custom-call(s32[14]{0:T(128)S(1)} %concatenate.27.sc, bf16[2,256,1024]{2,1,0:T(8,128)(2,1)} %collective-permute-done.18.g_ref, bf16[1,512,1024]{2,1,0:T(8,128)(2,1)S(1)} %copy-done.1, bf16[1,768,1024]{2,1,0:T(8,128)(2,1)} %k_ref.7, ...), custom_call_target="tpu_custom_call" | custom-call | flops 3355443200 | bytes 16777216 | tf_op jit(solution)/shard_map/pallas_call | solution.py:80
  228.1 3.9 %collective-permute-done.23.rest_4_ = bf16[1024,256]{1,0:T(8,128)(2,1)S(1)} collective-permute-done((bf16[1024,256]{1,0:T(8,128)(2,1)}, bf16[1024,256]{1,0:T(8,128)(2,1)S(1)}, u32[]{:S(2)}, u32[]{:S(2)}) %collective-permute-start.23) | collective-permute-done | bytes 524320 | tf_op jit(solution)/shard_map/ppermute | solution.py:196
  233.2 9.7 %collective-permute-done.30.rest_12_ = bf16[1024,256]{1,0:T(8,128)(2,1)S(1)} collective-permute-done((bf16[1024,256]{1,0:T(8,128)(2,1)}, bf16[1024,256]{1,0:T(8,128)(2,1)S(1)}, u32[]{:S(2)}, u32[]{:S(2)}) %collective-permute-start.30) | collective-permute-done | bytes 524320 | tf_op jit(solution)/shard_map/ppermute | solution.py:196
  243.2 10.4 %shard_map.132 = (bf16[2,256,1024]{2,1,0:T(8,128)(2,1)S(1)}, bf16[384,1024]{1,0:T(8,128)(2,1)S(1)}, bf16[384,1024]{1,0:T(8,128)(2,1)S(1)}) custom-call(s32[14]{0:T(128)S(1)} %concatenate.26.sc, bf16[2,256,1024]{2,1,0:T(8,128)(2,1)} %collective-permute-done.15.g_ref, bf16[1,512,1024]{2,1,0:T(8,128)(2,1)S(1)} %copy-done.1, bf16[1,768,1024]{2,1,0:T(8,128)(2,1)} %k_ref.7, ...), custom_call_target="tpu_custom_call" | custom-call | flops 3355443200 | bytes 16777216 | tf_op jit(solution)/shard_map/pallas_call | solution.py:80
  260.7 8.8 %collective-permute-done.32.rest_14_ = bf16[1024,256]{1,0:T(8,128)(2,1)S(1)} collective-permute-done((bf16[1024,256]{1,0:T(8,128)(2,1)S(1)}, bf16[1024,256]{1,0:T(8,128)(2,1)S(1)}, u32[]{:S(2)}, u32[]{:S(2)}) %collective-permute-start.32) | collective-permute-done | bytes 524320 | tf_op jit(solution)/shard_map/ppermute | solution.py:196
  273.5 7.6 %collective-permute-done.24.rest_5_ = bf16[1024,256]{1,0:T(8,128)(2,1)S(1)} collective-permute-done((bf16[1024,256]{1,0:T(8,128)(2,1)S(1)}, bf16[1024,256]{1,0:T(8,128)(2,1)S(1)}, u32[]{:S(2)}, u32[]{:S(2)}) %collective-permute-start.24) | collective-permute-done | bytes 524320 | tf_op jit(solution)/shard_map/ppermute | solution.py:200
  281.1 11.2 %collective-permute-done.31.rest_13_ = bf16[1024,256]{1,0:T(8,128)(2,1)S(1)} collective-permute-done((bf16[1024,256]{1,0:T(8,128)(2,1)S(1)}, bf16[1024,256]{1,0:T(8,128)(2,1)S(1)}, u32[]{:S(2)}, u32[]{:S(2)}) %collective-permute-start.31) | collective-permute-done | bytes 524320 | tf_op jit(solution)/shard_map/ppermute | solution.py:200
  292.3 11.2 %collective-permute-done.26.rest_7_ = bf16[1024,256]{1,0:T(8,128)(2,1)S(1)} collective-permute-done((bf16[1024,256]{1,0:T(8,128)(2,1)S(1)}, bf16[1024,256]{1,0:T(8,128)(2,1)S(1)}, u32[]{:S(2)}, u32[]{:S(2)}) %collective-permute-start.26) | collective-permute-done | bytes 524320 | tf_op jit(solution)/shard_map/ppermute | solution.py:200
  303.6 10.1 %collective-permute-done.33.rest_15_ = bf16[1024,256]{1,0:T(8,128)(2,1)S(1)} collective-permute-done((bf16[1024,256]{1,0:T(8,128)(2,1)S(1)}, bf16[1024,256]{1,0:T(8,128)(2,1)S(1)}, u32[]{:S(2)}, u32[]{:S(2)}) %collective-permute-start.33) | collective-permute-done | bytes 524320 | tf_op jit(solution)/shard_map/ppermute | solution.py:200
  314.5 11.4 %shard_map.135 = bf16[4,768,512]{2,1,0:T(8,128)(2,1)} custom-call(s32[8]{0:T(128)S(1)} %stack.35.sc, bf16[768,1024]{1,0:T(8,128)(2,1)} %pad_maximum_fusion.kg_ref, bf16[768,1024]{1,0:T(8,128)(2,1)} %pad_maximum_fusion.1.vg_ref, bf16[1024,256]{1,0:T(8,128)(2,1)} %bitcast.36.rest_0_, bf16[1024,256]{1,0:T(8,128)(2,1)} %collective-permute-done.20.rest_1_, ...), custom_call_target="tpu_custom_call" | custom-call | flops 6442450944 | bytes 14680064 | tf_op jit(solution)/shard_map/pallas_call | solution.py:128
  325.9 1.7 constant_dynamic-slice_fusion.1
  328.3 1.6 collective-permute-start.19
  331.6 1.6 collective-permute-start.35
  334.2 9.0 %collective-permute-done.19 = bf16[256,1024]{1,0:T(8,128)(2,1)S(1)} collective-permute-done((bf16[256,1024]{1,0:T(8,128)(2,1)S(1)}, bf16[256,1024]{1,0:T(8,128)(2,1)S(1)}, u32[]{:S(2)}, u32[]{:S(2)}) %collective-permute-start.19) | collective-permute-done | bytes 524320 | tf_op jit(solution)/shard_map/ppermute | solution.py:265
  343.1 1.6 fusion.5
  344.7 15.3 %collective-permute-done.35 = bf16[768,512]{1,0:T(8,128)(2,1)S(1)} collective-permute-done((bf16[768,512]{1,0:T(8,128)(2,1)S(1)}, bf16[768,512]{1,0:T(8,128)(2,1)S(1)}, u32[]{:S(2)}, u32[]{:S(2)}) %collective-permute-start.35) | collective-permute-done | bytes 786464 | tf_op jit(solution)/shard_map/ppermute | solution.py:281
  362.2 3.5 collective-permute-start.37
  365.7 5.1 %collective-permute-done.16 = bf16[256,1024]{1,0:T(8,128)(2,1)S(1)} collective-permute-done((bf16[256,1024]{1,0:T(8,128)(2,1)S(1)}, bf16[256,1024]{1,0:T(8,128)(2,1)S(1)}, u32[]{:S(2)}, u32[]{:S(2)}) %collective-permute-start.16) | collective-permute-done | bytes 524320 | tf_op jit(solution)/shard_map/ppermute | solution.py:265
  373.3 1.8 collective-permute-done.37.right_ref
  375.1 1.6 shard_map.137
  (165 shorter events, 43.5 us)
Async XLA Ops:
  0.6 18.1 %collective-permute-start.1 = (bf16[1024,256]{1,0:T(8,128)(2,1)}, bf16[1024,256]{1,0:T(8,128)(2,1)S(1)}, u32[]{:S(2)}, u32[]{:S(2)}) collective-permute-start(bf16[1024,256]{1,0:T(8,128)(2,1)} %bitcast.80), channel_id=1, source_target_pairs={{0,4},{2,6},{4,8},{6,10},{8,12},{10,14},{12,0},{14,2},{1,5},{3,7},... | collective-permute-start | bytes 1572872 | tf_op jit(solution)/shard_map/ppermute | solution.py:196
  3.7 26.3 %collective-permute-start.8 = (bf16[1024,256]{1,0:T(8,128)(2,1)}, bf16[1024,256]{1,0:T(8,128)(2,1)}, u32[]{:S(2)}, u32[]{:S(2)}) collective-permute-start(bf16[1024,256]{1,0:T(8,128)(2,1)} %bitcast.86), channel_id=1, source_target_pairs={{0,4},{2,6},{4,8},{6,10},{8,12},{10,14},{12,0},{14,2},{1,5},{3,7},... | collective-permute-start | bytes 1572872 | tf_op jit(solution)/shard_map/ppermute | solution.py:196
  18.7 22.6 %collective-permute-start.3 = (bf16[1024,256]{1,0:T(8,128)(2,1)S(1)}, bf16[1024,256]{1,0:T(8,128)(2,1)}, u32[]{:S(2)}, u32[]{:S(2)}) collective-permute-start(bf16[1024,256]{1,0:T(8,128)(2,1)S(1)} %collective-permute-done.1.rest_2_), channel_id=1, source_target_pairs={{0,4},{2,6},{4,8},{6,10},{8,12},{10,14},{12,0},{14,2},{1,5},{3,7},... | collective-permute-start | bytes 1572872 | tf_op jit(solution)/shard_map/ppermute | solution.py:196
  30.0 22.5 %collective-permute-start.10 = (bf16[1024,256]{1,0:T(8,128)(2,1)}, bf16[1024,256]{1,0:T(8,128)(2,1)}, u32[]{:S(2)}, u32[]{:S(2)}) collective-permute-start(bf16[1024,256]{1,0:T(8,128)(2,1)} %collective-permute-done.8.rest_10_), channel_id=1, source_target_pairs={{0,4},{2,6},{4,8},{6,10},{8,12},{10,14},{12,0},{14,2},{1,5},{3,7},... | collective-permute-start | bytes 1572872 | tf_op jit(solution)/shard_map/ppermute | solution.py:196
  30.1 22.5 %collective-permute-start = (bf16[1024,256]{1,0:T(8,128)(2,1)}, bf16[1024,256]{1,0:T(8,128)(2,1)S(1)}, u32[]{:S(2)}, u32[]{:S(2)}) collective-permute-start(bf16[1024,256]{1,0:T(8,128)(2,1)} %bitcast.81), channel_id=1, source_target_pairs={{0,2},{2,0},{4,6},{6,4},{8,10},{10,8},{12,14},{14,12},{1,3},{3,1},... | collective-permute-start | bytes 1572872 | tf_op jit(solution)/shard_map/ppermute | solution.py:200
  31.8 24.6 %collective-permute-start.7 = (bf16[1024,256]{1,0:T(8,128)(2,1)}, bf16[1024,256]{1,0:T(8,128)(2,1)S(1)}, u32[]{:S(2)}, u32[]{:S(2)}) collective-permute-start(bf16[1024,256]{1,0:T(8,128)(2,1)} %bitcast.87), channel_id=1, source_target_pairs={{0,2},{2,0},{4,6},{6,4},{8,10},{10,8},{12,14},{14,12},{1,3},{3,1},... | collective-permute-start | bytes 1572872 | tf_op jit(solution)/shard_map/ppermute | solution.py:200
  32.1 35.5 %collective-permute-start.2 = (bf16[1024,256]{1,0:T(8,128)(2,1)S(1)}, bf16[1024,256]{1,0:T(8,128)(2,1)S(1)}, u32[]{:S(2)}, u32[]{:S(2)}) collective-permute-start(bf16[1024,256]{1,0:T(8,128)(2,1)S(1)} %collective-permute-done.1.rest_2_), channel_id=1, source_target_pairs={{0,2},{2,0},{4,6},{6,4},{8,10},{10,8},{12,14},{14,12},{1,3},{3,1},... | collective-permute-start | bytes 1572872 | tf_op jit(solution)/shard_map/ppermute | solution.py:200
  41.3 28.9 %collective-permute-start.5 = (bf16[1024,256]{1,0:T(8,128)(2,1)}, bf16[1024,256]{1,0:T(8,128)(2,1)}, u32[]{:S(2)}, u32[]{:S(2)}) collective-permute-start(bf16[1024,256]{1,0:T(8,128)(2,1)} %collective-permute-done.3.rest_4_), channel_id=1, source_target_pairs={{0,4},{2,6},{4,8},{6,10},{8,12},{10,14},{12,0},{14,2},{1,5},{3,7},... | collective-permute-start | bytes 1572872 | tf_op jit(solution)/shard_map/ppermute | solution.py:196
  52.5 21.6 %collective-permute-start.12 = (bf16[1024,256]{1,0:T(8,128)(2,1)}, bf16[1024,256]{1,0:T(8,128)(2,1)}, u32[]{:S(2)}, u32[]{:S(2)}) collective-permute-start(bf16[1024,256]{1,0:T(8,128)(2,1)} %collective-permute-done.10.rest_12_), channel_id=1, source_target_pairs={{0,4},{2,6},{4,8},{6,10},{8,12},{10,14},{12,0},{14,2},{1,5},{3,7},... | collective-permute-start | bytes 1572872 | tf_op jit(solution)/shard_map/ppermute | solution.py:196
  53.3 30.7 %collective-permute-start.9 = (bf16[1024,256]{1,0:T(8,128)(2,1)}, bf16[1024,256]{1,0:T(8,128)(2,1)}, u32[]{:S(2)}, u32[]{:S(2)}) collective-permute-start(bf16[1024,256]{1,0:T(8,128)(2,1)} %collective-permute-done.8.rest_10_), channel_id=1, source_target_pairs={{0,2},{2,0},{4,6},{6,4},{8,10},{10,8},{12,14},{14,12},{1,3},{3,1},... | collective-permute-start | bytes 1572872 | tf_op jit(solution)/shard_map/ppermute | solution.py:200
  57.2 33.0 %collective-permute-start.4 = (bf16[1024,256]{1,0:T(8,128)(2,1)}, bf16[1024,256]{1,0:T(8,128)(2,1)}, u32[]{:S(2)}, u32[]{:S(2)}) collective-permute-start(bf16[1024,256]{1,0:T(8,128)(2,1)} %collective-permute-done.3.rest_4_), channel_id=1, source_target_pairs={{0,2},{2,0},{4,6},{6,4},{8,10},{10,8},{12,14},{14,12},{1,3},{3,1},... | collective-permute-start | bytes 1572872 | tf_op jit(solution)/shard_map/ppermute | solution.py:200
  68.4 33.0 %collective-permute-start.11 = (bf16[1024,256]{1,0:T(8,128)(2,1)}, bf16[1024,256]{1,0:T(8,128)(2,1)}, u32[]{:S(2)}, u32[]{:S(2)}) collective-permute-start(bf16[1024,256]{1,0:T(8,128)(2,1)} %collective-permute-done.10.rest_12_), channel_id=1, source_target_pairs={{0,2},{2,0},{4,6},{6,4},{8,10},{10,8},{12,14},{14,12},{1,3},{3,1},... | collective-permute-start | bytes 1572872 | tf_op jit(solution)/shard_map/ppermute | solution.py:200
  70.1 42.5 %collective-permute-start.6 = (bf16[1024,256]{1,0:T(8,128)(2,1)}, bf16[1024,256]{1,0:T(8,128)(2,1)}, u32[]{:S(2)}, u32[]{:S(2)}) collective-permute-start(bf16[1024,256]{1,0:T(8,128)(2,1)} %collective-permute-done.5.rest_6_), channel_id=1, source_target_pairs={{0,2},{2,0},{4,6},{6,4},{8,10},{10,8},{12,14},{14,12},{1,3},{3,1},... | collective-permute-start | bytes 1572872 | tf_op jit(solution)/shard_map/ppermute | solution.py:200
  74.1 47.1 %collective-permute-start.13 = (bf16[1024,256]{1,0:T(8,128)(2,1)}, bf16[1024,256]{1,0:T(8,128)(2,1)}, u32[]{:S(2)}, u32[]{:S(2)}) collective-permute-start(bf16[1024,256]{1,0:T(8,128)(2,1)} %collective-permute-done.12.rest_14_), channel_id=1, source_target_pairs={{0,2},{2,0},{4,6},{6,4},{8,10},{10,8},{12,14},{14,12},{1,3},{3,1},... | collective-permute-start | bytes 1572872 | tf_op jit(solution)/shard_map/ppermute | solution.py:200
  79.6 41.7 %copy-start = (bf16[1,768,1024]{2,1,0:T(8,128)(2,1)S(1)}, bf16[1,768,1024]{2,1,0:T(8,128)(2,1)}, u32[]{:S(2)}) copy-start(bf16[1,768,1024]{2,1,0:T(8,128)(2,1)} %k_ref.7) | copy-start | bytes 4718596
  79.6 41.6 %copy-start.1 = (bf16[1,512,1024]{2,1,0:T(8,128)(2,1)S(1)}, bf16[1,512,1024]{2,1,0:T(8,128)(2,1)}, u32[]{:S(2)}) copy-start(bf16[1,512,1024]{2,1,0:T(8,128)(2,1)} %q_ref.7) | copy-start | bytes 3145732
  79.7 41.6 %copy-start.2 = (bf16[1,1024,256]{2,1,0:T(8,128)(2,1)S(1)}, bf16[1,1024,256]{2,1,0:T(8,128)(2,1)}, u32[]{:S(2)}) copy-start(bf16[1,1024,256]{2,1,0:T(8,128)(2,1)} %param.19) | copy-start | bytes 1572868
  137.8 45.0 %copy-start.31 = (bf16[512,2,1024]{2,0,1:T(8,128)(2,1)S(1)}, bf16[512,2,1024]{2,0,1:T(8,128)(2,1)}, u32[]{:S(2)}) copy-start(bf16[512,2,1024]{2,0,1:T(8,128)(2,1)} %copy.19) | copy-start | bytes 6291460
  137.8 26.1 %collective-permute-start.14 = (bf16[2,256,1024]{2,1,0:T(8,128)(2,1)S(1)}, bf16[2,256,1024]{2,1,0:T(8,128)(2,1)S(1)}, u32[]{:S(2)}, u32[]{:S(2)}) collective-permute-start(bf16[2,256,1024]{2,1,0:T(8,128)(2,1)S(1)} %get-tuple-element.17), channel_id=1, source_target_pairs={{0,1},{1,0},{2,3},{3,2},{4,5},{5,4},{6,7},{7,6},{8,9},{9,8},{10,11... | collective-permute-start | bytes 3145736 | tf_op jit(solution)/shard_map/ppermute | solution.py:256
  149.4 40.5 %copy-start.34 = (s32[16,3]{0,1:T(4,128)S(1)}, s32[16,3]{0,1:T(4,128)}, u32[]{:S(2)}) copy-start(s32[16,3]{0,1:T(4,128)} %param.23) | copy-start | bytes 580
  149.5 66.0 %copy-start.5 = (bf16[1,1024,256]{2,1,0:T(8,128)(2,1)S(1)}, bf16[1,1024,256]{2,1,0:T(8,128)(2,1)}, u32[]{:S(2)}) copy-start(bf16[1,1024,256]{2,1,0:T(8,128)(2,1)} %param.16) | copy-start | bytes 1572868
  149.5 66.0 %copy-start.9 = (bf16[1024,256]{1,0:T(8,128)(2,1)S(1)}, bf16[1024,256]{1,0:T(8,128)(2,1)}, u32[]{:S(2)}) copy-start(bf16[1024,256]{1,0:T(8,128)(2,1)} %copy-done.6) | copy-start | bytes 1572868
  149.5 66.0 %copy-start.12 = (bf16[1024,256]{1,0:T(8,128)(2,1)S(1)}, bf16[1024,256]{1,0:T(8,128)(2,1)}, u32[]{:S(2)}) copy-start(bf16[1024,256]{1,0:T(8,128)(2,1)} %copy-done.10) | copy-start | bytes 1572868
  149.5 33.3 %collective-permute-start.17 = (bf16[2,256,1024]{2,1,0:T(8,128)(2,1)S(1)}, bf16[2,256,1024]{2,1,0:T(8,128)(2,1)S(1)}, u32[]{:S(2)}, u32[]{:S(2)}) collective-permute-start(bf16[2,256,1024]{2,1,0:T(8,128)(2,1)S(1)} %get-tuple-element.19), channel_id=1, source_target_pairs={{0,1},{1,0},{2,3},{3,2},{4,5},{5,4},{6,7},{7,6},{8,9},{9,8},{10,11... | collective-permute-start | bytes 3145736 | tf_op jit(solution)/shard_map/ppermute | solution.py:256
  185.7 29.5 %collective-permute-start.18 = (bf16[2,256,1024]{2,1,0:T(8,128)(2,1)}, bf16[2,256,1024]{2,1,0:T(8,128)(2,1)}, u32[]{:S(2)}, u32[]{:S(2)}) collective-permute-start(bf16[2,256,1024]{2,1,0:T(8,128)(2,1)} %get-tuple-element.35), channel_id=1, source_target_pairs={{16,0},{17,1},{18,2},{19,3},{20,4},{21,5},{22,6},{23,7},{24,8},{25... | collective-permute-start | bytes 3145736 | tf_op jit(solution)/shard_map/ppermute | solution.py:259
  187.0 67.8 %collective-permute-start.20 = (bf16[1024,256]{1,0:T(8,128)(2,1)}, bf16[1024,256]{1,0:T(8,128)(2,1)}, u32[]{:S(2)}, u32[]{:S(2)}) collective-permute-start(bf16[1024,256]{1,0:T(8,128)(2,1)} %bitcast.36.rest_0_), channel_id=1, source_target_pairs={{0,2},{2,0},{4,6},{6,4},{8,10},{10,8},{12,14},{14,12},{1,3},{3,1},... | collective-permute-start | bytes 1572872 | tf_op jit(solution)/shard_map/ppermute | solution.py:200
  187.8 16.1 %collective-permute-start.21 = (bf16[1024,256]{1,0:T(8,128)(2,1)}, bf16[1024,256]{1,0:T(8,128)(2,1)}, u32[]{:S(2)}, u32[]{:S(2)}) collective-permute-start(bf16[1024,256]{1,0:T(8,128)(2,1)} %bitcast.36.rest_0_), channel_id=1, source_target_pairs={{0,4},{2,6},{4,8},{6,10},{8,12},{10,14},{12,0},{14,2},{1,5},{3,7},... | collective-permute-start | bytes 1572872 | tf_op jit(solution)/shard_map/ppermute | solution.py:196
  188.3 26.9 %collective-permute-start.28 = (bf16[1024,256]{1,0:T(8,128)(2,1)}, bf16[1024,256]{1,0:T(8,128)(2,1)}, u32[]{:S(2)}, u32[]{:S(2)}) collective-permute-start(bf16[1024,256]{1,0:T(8,128)(2,1)} %bitcast.37.rest_8_), channel_id=1, source_target_pairs={{0,4},{2,6},{4,8},{6,10},{8,12},{10,14},{12,0},{14,2},{1,5},{3,7},... | collective-permute-start | bytes 1572872 | tf_op jit(solution)/shard_map/ppermute | solution.py:196
  190.3 52.6 %collective-permute-start.15 = (bf16[2,256,1024]{2,1,0:T(8,128)(2,1)}, bf16[2,256,1024]{2,1,0:T(8,128)(2,1)}, u32[]{:S(2)}, u32[]{:S(2)}) collective-permute-start(bf16[2,256,1024]{2,1,0:T(8,128)(2,1)} %get-tuple-element.34), channel_id=1, source_target_pairs={{16,0},{17,1},{18,2},{19,3},{20,4},{21,5},{22,6},{23,7},{24,8},{25... | collective-permute-start | bytes 3145736 | tf_op jit(solution)/shard_map/ppermute | solution.py:259
  204.0 52.1 %collective-permute-start.27 = (bf16[1024,256]{1,0:T(8,128)(2,1)}, bf16[1024,256]{1,0:T(8,128)(2,1)S(1)}, u32[]{:S(2)}, u32[]{:S(2)}) collective-permute-start(bf16[1024,256]{1,0:T(8,128)(2,1)} %bitcast.37.rest_8_), channel_id=1, source_target_pairs={{0,2},{2,0},{4,6},{6,4},{8,10},{10,8},{12,14},{14,12},{1,3},{3,1},... | collective-permute-start | bytes 1572872 | tf_op jit(solution)/shard_map/ppermute | solution.py:200
  215.2 16.7 %collective-permute-start.23 = (bf16[1024,256]{1,0:T(8,128)(2,1)}, bf16[1024,256]{1,0:T(8,128)(2,1)S(1)}, u32[]{:S(2)}, u32[]{:S(2)}) collective-permute-start(bf16[1024,256]{1,0:T(8,128)(2,1)} %collective-permute-done.21.rest_2_), channel_id=1, source_target_pairs={{0,4},{2,6},{4,8},{6,10},{8,12},{10,14},{12,0},{14,2},{1,5},{3,7},... | collective-permute-start | bytes 1572872 | tf_op jit(solution)/shard_map/ppermute | solution.py:196
  215.2 27.7 %collective-permute-start.30 = (bf16[1024,256]{1,0:T(8,128)(2,1)}, bf16[1024,256]{1,0:T(8,128)(2,1)S(1)}, u32[]{:S(2)}, u32[]{:S(2)}) collective-permute-start(bf16[1024,256]{1,0:T(8,128)(2,1)} %collective-permute-done.28.rest_10_), channel_id=1, source_target_pairs={{0,4},{2,6},{4,8},{6,10},{8,12},{10,14},{12,0},{14,2},{1,5},{3,7},... | collective-permute-start | bytes 1572872 | tf_op jit(solution)/shard_map/ppermute | solution.py:196
  231.9 24.9 %collective-permute-start.22 = (bf16[1024,256]{1,0:T(8,128)(2,1)}, bf16[1024,256]{1,0:T(8,128)(2,1)S(1)}, u32[]{:S(2)}, u32[]{:S(2)}) collective-permute-start(bf16[1024,256]{1,0:T(8,128)(2,1)} %collective-permute-done.21.rest_2_), channel_id=1, source_target_pairs={{0,2},{2,0},{4,6},{6,4},{8,10},{10,8},{12,14},{14,12},{1,3},{3,1},... | collective-permute-start | bytes 1572872 | tf_op jit(solution)/shard_map/ppermute | solution.py:200
  242.9 16.6 %collective-permute-start.25 = (bf16[1024,256]{1,0:T(8,128)(2,1)S(1)}, bf16[1024,256]{1,0:T(8,128)(2,1)S(1)}, u32[]{:S(2)}, u32[]{:S(2)}) collective-permute-start(bf16[1024,256]{1,0:T(8,128)(2,1)S(1)} %collective-permute-done.23.rest_4_), channel_id=1, source_target_pairs={{0,4},{2,6},{4,8},{6,10},{8,12},{10,14},{12,0},{14,2},{1,5},{3,7},... | collective-permute-start | bytes 1572872 | tf_op jit(solution)/shard_map/ppermute | solution.py:196
  242.9 26.7 %collective-permute-start.32 = (bf16[1024,256]{1,0:T(8,128)(2,1)S(1)}, bf16[1024,256]{1,0:T(8,128)(2,1)S(1)}, u32[]{:S(2)}, u32[]{:S(2)}) collective-permute-start(bf16[1024,256]{1,0:T(8,128)(2,1)S(1)} %collective-permute-done.30.rest_12_), channel_id=1, source_target_pairs={{0,4},{2,6},{4,8},{6,10},{8,12},{10,14},{12,0},{14,2},{1,5},{3,7},... | collective-permute-start | bytes 1572872 | tf_op jit(solution)/shard_map/ppermute | solution.py:196
  254.8 18.8 %collective-permute-start.29 = (bf16[1024,256]{1,0:T(8,128)(2,1)}, bf16[1024,256]{1,0:T(8,128)(2,1)S(1)}, u32[]{:S(2)}, u32[]{:S(2)}) collective-permute-start(bf16[1024,256]{1,0:T(8,128)(2,1)} %collective-permute-done.28.rest_10_), channel_id=1, source_target_pairs={{0,2},{2,0},{4,6},{6,4},{8,10},{10,8},{12,14},{14,12},{1,3},{3,1},... | collective-permute-start | bytes 1572872 | tf_op jit(solution)/shard_map/ppermute | solution.py:200
  256.1 25.0 %collective-permute-start.24 = (bf16[1024,256]{1,0:T(8,128)(2,1)S(1)}, bf16[1024,256]{1,0:T(8,128)(2,1)S(1)}, u32[]{:S(2)}, u32[]{:S(2)}) collective-permute-start(bf16[1024,256]{1,0:T(8,128)(2,1)S(1)} %collective-permute-done.23.rest_4_), channel_id=1, source_target_pairs={{0,2},{2,0},{4,6},{6,4},{8,10},{10,8},{12,14},{14,12},{1,3},{3,1},... | collective-permute-start | bytes 1572872 | tf_op jit(solution)/shard_map/ppermute | solution.py:200
  256.9 35.5 %collective-permute-start.31 = (bf16[1024,256]{1,0:T(8,128)(2,1)S(1)}, bf16[1024,256]{1,0:T(8,128)(2,1)S(1)}, u32[]{:S(2)}, u32[]{:S(2)}) collective-permute-start(bf16[1024,256]{1,0:T(8,128)(2,1)S(1)} %collective-permute-done.30.rest_12_), channel_id=1, source_target_pairs={{0,2},{2,0},{4,6},{6,4},{8,10},{10,8},{12,14},{14,12},{1,3},{3,1},... | collective-permute-start | bytes 1572872 | tf_op jit(solution)/shard_map/ppermute | solution.py:200
  259.5 44.1 %collective-permute-start.26 = (bf16[1024,256]{1,0:T(8,128)(2,1)S(1)}, bf16[1024,256]{1,0:T(8,128)(2,1)S(1)}, u32[]{:S(2)}, u32[]{:S(2)}) collective-permute-start(bf16[1024,256]{1,0:T(8,128)(2,1)S(1)} %collective-permute-done.25.rest_6_), channel_id=1, source_target_pairs={{0,2},{2,0},{4,6},{6,4},{8,10},{10,8},{12,14},{14,12},{1,3},{3,1},... | collective-permute-start | bytes 1572872 | tf_op jit(solution)/shard_map/ppermute | solution.py:200
  269.6 44.1 %collective-permute-start.33 = (bf16[1024,256]{1,0:T(8,128)(2,1)S(1)}, bf16[1024,256]{1,0:T(8,128)(2,1)S(1)}, u32[]{:S(2)}, u32[]{:S(2)}) collective-permute-start(bf16[1024,256]{1,0:T(8,128)(2,1)S(1)} %collective-permute-done.32.rest_14_), channel_id=1, source_target_pairs={{0,2},{2,0},{4,6},{6,4},{8,10},{10,8},{12,14},{14,12},{1,3},{3,1},... | collective-permute-start | bytes 1572872 | tf_op jit(solution)/shard_map/ppermute | solution.py:200
  273.5 40.1 %copy-start.40 = (bf16[1024,256]{1,0:T(8,128)(2,1)}, bf16[1024,256]{1,0:T(8,128)(2,1)S(1)}, u32[]{:S(2)}) copy-start(bf16[1024,256]{1,0:T(8,128)(2,1)S(1)} %collective-permute-done.29.rest_11_) | copy-start | bytes 1572868
  327.6 3.5 collective-permute-start.34
  328.3 14.8 %collective-permute-start.19 = (bf16[256,1024]{1,0:T(8,128)(2,1)S(1)}, bf16[256,1024]{1,0:T(8,128)(2,1)S(1)}, u32[]{:S(2)}, u32[]{:S(2)}) collective-permute-start(bf16[256,1024]{1,0:T(8,128)(2,1)S(1)} %dynamic-slice_bitcast_fusion.1), channel_id=1, source_target_pairs={{0,1},{1,0},{2,3},{3,2},{4,5},{5,4},{6,7},{7,6},{8,9},{9,8},{10,11... | collective-permute-start | bytes 1572872 | tf_op jit(solution)/shard_map/ppermute | solution.py:265
  331.6 28.4 %collective-permute-start.35 = (bf16[768,512]{1,0:T(8,128)(2,1)S(1)}, bf16[768,512]{1,0:T(8,128)(2,1)S(1)}, u32[]{:S(2)}, u32[]{:S(2)}) collective-permute-start(bf16[768,512]{1,0:T(8,128)(2,1)S(1)} %get-tuple-element.36), channel_id=1, source_target_pairs={{0,1},{1,0},{2,3},{3,2},{4,5},{5,4},{6,7},{7,6},{8,9},{9,8},{10,11... | collective-permute-start | bytes 2359304 | tf_op jit(solution)/shard_map/ppermute | solution.py:281
  333.3 37.5 %collective-permute-start.16 = (bf16[256,1024]{1,0:T(8,128)(2,1)S(1)}, bf16[256,1024]{1,0:T(8,128)(2,1)S(1)}, u32[]{:S(2)}, u32[]{:S(2)}) collective-permute-start(bf16[256,1024]{1,0:T(8,128)(2,1)S(1)} %dynamic-slice_bitcast_fusion.2), channel_id=1, source_target_pairs={{0,1},{1,0},{2,3},{3,2},{4,5},{5,4},{6,7},{7,6},{8,9},{9,8},{10,11... | collective-permute-start | bytes 1572872 | tf_op jit(solution)/shard_map/ppermute | solution.py:265
  334.2 36.6 %copy-start.33 = (bf16[2,256,1024]{2,1,0:T(8,128)(2,1)S(1)}, bf16[2,256,1024]{2,1,0:T(8,128)(2,1)}, u32[]{:S(2)}) copy-start(bf16[2,256,1024]{2,1,0:T(8,128)(2,1)} %get-tuple-element.34) | copy-start | bytes 3145732
  361.0 12.3 %collective-permute-start.36 = (bf16[2,128,512]{2,1,0:T(8,128)(2,1)S(1)}, bf16[2,128,512]{2,1,0:T(8,128)(2,1)S(1)}, u32[]{:S(2)}, u32[]{:S(2)}) collective-permute-start(bf16[2,128,512]{2,1,0:T(8,128)(2,1)S(1)} %get-tuple-element.29), channel_id=1, source_target_pairs={{0,2},{2,4},{4,6},{6,8},{8,10},{10,12},{12,14},{14,0},{1,3},{3,5},... | collective-permute-start | bytes 786440 | tf_op jit(solution)/shard_map/ppermute | solution.py:330
  362.2 12.9 %collective-permute-start.37 = (bf16[2,128,512]{2,1,0:T(8,128)(2,1)S(1)}, bf16[2,128,512]{2,1,0:T(8,128)(2,1)S(1)}, u32[]{:S(2)}, u32[]{:S(2)}) collective-permute-start(bf16[2,128,512]{2,1,0:T(8,128)(2,1)S(1)} %get-tuple-element.31), channel_id=1, source_target_pairs={{2,0},{4,2},{6,4},{8,6},{10,8},{12,10},{14,12},{0,14},{3,1},{5,3},... | collective-permute-start | bytes 786440 | tf_op jit(solution)/shard_map/ppermute | solution.py:331
  (33 other events, 286.8 us)

commit v3 on v2

--- a/solution.py
+++ b/solution.py
@@ -179,27 +179,249 @@
     )(scalars, *arrays)
 
 
-def gathered(shard, factors):
-    count = lax.axis_size("dp")
-    me = lax.axis_index("dp")
-    if shard.shape[1] != BLOCK or factors is None:
-        full = lax.all_gather(shard, "dp", axis=1, tiled=True)
-        blocks = [full[:, i : i + BLOCK] for i in range(0, full.shape[1], BLOCK)]
-        return blocks, list(jnp.arange(len(blocks), dtype=jnp.int32))
-    outer, inner = factors
-    ring = [(i, (i + inner) % count) for i in range(count)]
-    swap = [(i, i ^ 1) for i in range(count)]
-    blocks, sources = [], []
-    block = shard
+def gathered(shard):
+    full = lax.all_gather(shard, "dp", axis=1, tiled=True)
+    blocks = [full[:, i : i + BLOCK] for i in range(0, full.shape[1], BLOCK)]
+    return blocks, list(jnp.arange(len(blocks), dtype=jnp.int32))
+
+
+def fused_kernel(dims, sc, top_ref, q_ref, k_ref, v_ref, wo_ref, wq_ref, wk_ref, wv_ref,
+                 sections_ref, parts_ref, wbuf, kg, vg, acc, mixed, other, section, incoming,
+                 zs, zr, xs, xr, ms, mr, ss, sr):
+    q_rows, k_rows, outer, heads = dims
+    half = acc.shape[2]
+    per = half // BLOCK
+    scale = DH ** (-0.5)
+    seg, me, mp = lax.axis_index("segment"), lax.axis_index("dp"), lax.axis_index("mp")
+    z, x = me // 2, me % 2
+    up = ((z + 1) % outer) * 2 + x
+    down = ((z + outer - 1) % outer) * 2 + x
+    side = z * 2 + 1 - x
+    weights = (wo_ref, wq_ref, wk_ref, wv_ref)
+    mesh_id = pl.DeviceIdType.MESH
+
+    barrier = pltpu.get_barrier_semaphore()
+    for peer in ((seg, up, mp), (seg, down, mp), (seg, side, mp), (seg, me, 1 - mp), (1 - seg, me, mp)):
+        pl.semaphore_signal(barrier, inc=1, device_id=peer, device_id_type=mesh_id)
+    pl.semaphore_wait(barrier, 5)
+
+    def block(w, r, sx):
+        return weights[w].at[0] if r == 0 and sx == 0 else wbuf.at[w, r * 2 + sx]
+
+    def source(r, sx):
+        return ((z + outer - r) % outer) * 2 + (x if sx == 0 else 1 - x)
+
+    def send(src, dst, a, b, peer):
+        return pltpu.make_async_remote_copy(
+            src_ref=src, dst_ref=dst, send_sem=a, recv_sem=b, device_id=peer, device_id_type=mesh_id
+        )
+
+    def z_copy(w, r):
+        return send(block(w, r, 0), block(w, r + 1, 0), zs.at[w, r], zr.at[w, r], (seg, up, mp))
+
+    def x_copy(w, r):
+        return send(block(w, r, 0), block(w, r, 1), xs.at[w, r], xr.at[w, r], (seg, side, mp))
+
+    def advance(pair, r):
+        for w in pair:
+            if r > 0:
+                z_copy(w, r - 1).wait_recv()
+            if r < outer - 1:
+                z_copy(w, r).start()
+            x_copy(w, r).start()
+
+    def arrive(pair):
+        for w in pair:
+            for r in range(outer):
+                x_copy(w, r).wait_recv()
+
+    slots = [(r, sx) for r in range(outer) for sx in range(2)]
+
+    def tick(s, grad):
+        acc[...] = jnp.zeros_like(acc)
+
+        def one_head(h, carry):
+            hs = pl.ds(pl.multiple_of(h * DH, DH), DH)
+            og = jnp.zeros((q_rows, DH), F32)
+            for r, sx in slots:
+                og += dot(grad(source(r, sx)), block(0, r, sx)[hs, :], 1, 1)
+            og = og.astype(BF16)
+            q = q_ref[0, s * q_rows : (s + 1) * q_rows, hs]
+            k = k_ref[0, s * k_rows : (s + 1) * k_rows, hs]
+            v = v_ref[0, s * k_rows : (s + 1) * k_rows, hs]
+            scores = dot(q, k, 1, 1) * scale
+            rows = lax.broadcasted_iota(jnp.int32, scores.shape, 0)
+            cols = lax.broadcasted_iota(jnp.int32, scores.shape, 1)
+            allowed = None
+            for e in range(2):
+                q_len, k_off, k_len = sc[s, e], sc[s, 2 + e] * TILE, sc[s, 4 + e]
+                hit = (rows >= e * TILE) & (rows < e * TILE + q_len)
+                hit = hit & (cols >= k_off) & (cols < k_off + k_len)
+                allowed = hit if allowed is None else allowed | hit
+            masked = jnp.where(allowed, scores, masked_floor)
+            peak = jnp.max(masked, axis=-1, keepdims=True)
+            terms = jnp.where(allowed, jnp.exp(masked - peak), 0.0)
+            prob = terms / jnp.maximum(jnp.sum(terms, axis=-1, keepdims=True), 1.0)
+            prob_bf = prob.astype(BF16)
+            attended = dot(prob_bf, v, 1, 0)
+            out_dot = jnp.sum(og.astype(F32) * attended, axis=-1, keepdims=True)
+            sg = (prob * (dot(og, v, 1, 1) - out_dot)).astype(BF16)
+            qg = (dot(sg, k, 1, 0) * scale).astype(BF16)
+            kg[s * k_rows : (s + 1) * k_rows, hs] = (dot(sg, q, 0, 0) * scale).astype(BF16)
+            vg[s * k_rows : (s + 1) * k_rows, hs] = dot(prob_bf, og, 0, 0).astype(BF16)
+            for r, sx in slots:
+                src = source(r, sx)
+                at = pl.ds(pl.multiple_of((src % per) * BLOCK, BLOCK), BLOCK)
+                acc[src // per, :, at] += dot(qg, block(1, r, sx)[hs, :], 1, 0)
+            return carry
+
+        lax.fori_loop(0, heads, one_head, 0)
+        mixed[s] = acc[...].astype(BF16)
+
+    def top_block(s):
+        def load(src):
+            at = pl.ds(pl.multiple_of(src * BLOCK, BLOCK), BLOCK)
+            return top_ref[s * q_rows : (s + 1) * q_rows, at]
+
+        return load
+
+    def incoming_block(s):
+        def load(src):
+            at = pl.ds(pl.multiple_of((src % per) * BLOCK, BLOCK), BLOCK)
+            return incoming[s, src // per, :, at]
+
+        return load
+
+    def upper_copy(s):
+        return send(mixed.at[s], other.at[s], ms.at[0, s], mr.at[0, s], (seg, me, 1 - mp))
+
+    def lower_copy(s):
+        return send(mixed.at[s, 1 - mp], other.at[s, 0], ms.at[1, s], mr.at[1, s], (seg, me, 1 - mp))
+
+    def layer_copy(s):
+        return send(section.at[s], incoming.at[s], ss.at[s], sr.at[s], (1 - seg, me, mp))
+
+    def finish_upper(s):
+        upper_copy(s).wait_recv()
+        rows = slice(s * q_rows, (s + 1) * q_rows)
+        for i in range(2):
+            base = top_ref[rows, i * half : (i + 1) * half].astype(F32)
+            total = base + (mixed[s, i].astype(F32) + other[s, i].astype(F32))
+            section[s, i] = total.astype(BF16)
+        layer_copy(s).start()
+        sections_ref[0, rows, :] = section[s, mp]
+
+    def finish_lower(s):
+        lower_copy(s).wait_recv()
+        rows = slice(s * q_rows, (s + 1) * q_rows)
+        total = mixed[s, mp].astype(F32) + other[s, 0].astype(F32)
+        sections_ref[0, rows, :] = (incoming[s, mp].astype(F32) + total).astype(BF16)
+
     for r in range(outer):
-        if r:
-            block = lax.ppermute(block, "dp", ring)
-        source = (me - r * inner + count) % count
-        blocks.append(block)
-        sources.append(source)
-        blocks.append(lax.ppermute(block, "dp", swap))
-        sources.append(source ^ 1)
-    return blocks, sources
+        advance((0, 1), r)
+    advance((2, 3), 0)
+    arrive((0, 1))
+
+    @pl.when(seg == 1)
+    def _():
+        tick(0, top_block(0))
+        upper_copy(0).start()
+
+    advance((2, 3), 1)
+
+    @pl.when(seg == 1)
+    def _():
+        tick(1, top_block(1))
+        upper_copy(1).start()
+        finish_upper(0)
+
+    for r in range(2, outer - 1):
+        advance((2, 3), r)
+
+    @pl.when(seg == 1)
+    def _():
+        finish_upper(1)
+
+    @pl.when(seg == 0)
+    def _():
+        layer_copy(0).wait_recv()
+        tick(0, incoming_block(0))
+        lower_copy(0).start()
+
+    advance((2, 3), outer - 1)
+
+    @pl.when(seg == 0)
+    def _():
+        layer_copy(1).wait_recv()
+        tick(1, incoming_block(1))
+        lower_copy(1).start()
+        finish_lower(0)
+
+    arrive((2, 3))
+    quarter = parts_ref.shape[2]
+    step = 256
+
+    def encode(i, carry):
+        rows = pl.ds(pl.multiple_of(i * step, step), step)
+        for r, sx in slots:
+            src = source(r, sx)
+            each = quarter // BLOCK
+            at = pl.ds(pl.multiple_of((src % each) * BLOCK, BLOCK), BLOCK)
+            part = dot(kg[rows, :], block(2, r, sx)[...], 1, 0)
+            part += dot(vg[rows, :], block(3, r, sx)[...], 1, 0)
+            parts_ref[src // each, rows, at] = part.astype(BF16)
+        return carry
+
+    lax.fori_loop(0, kg.shape[0] // step, encode, 0)
+
+    @pl.when(seg == 0)
+    def _():
+        finish_lower(1)
+        for s in range(2):
+            lower_copy(s).wait_send()
+
+    @pl.when(seg == 1)
+    def _():
+        for s in range(2):
+            upper_copy(s).wait_send()
+            layer_copy(s).wait_send()
+
+    for w in range(4):
+        for r in range(outer):
+            x_copy(w, r).wait_send()
+            if r < outer - 1:
+                z_copy(w, r).wait_send()
+
+
+def run_fused(scalars, top, q, k, v, wo, wq, wk, wv, outer):
+    micro = scalars.shape[0]
+    q_rows, k_rows = top.shape[0] // micro, k.shape[1] // micro
+    width, depth = top.shape[1], q.shape[2]
+    half = width // 2
+    vmem = pl.BlockSpec(memory_space=pltpu.VMEM)
+    dma = pltpu.SemaphoreType.DMA
+    return pl.pallas_call(
+        functools.partial(fused_kernel, (q_rows, k_rows, outer, depth // DH)),
+        in_specs=[pl.BlockSpec(memory_space=pltpu.SMEM)] + [vmem] * 8,
+        out_specs=[vmem, vmem],
+        out_shape=[
+            jax.ShapeDtypeStruct((1, micro * q_rows, half), BF16),
+            jax.ShapeDtypeStruct((4, micro * k_rows, width // 4), BF16),
+        ],
+        scratch_shapes=[
+            pltpu.VMEM((4, 2 * outer, depth, BLOCK), BF16),
+            pltpu.VMEM((micro * k_rows, depth), BF16),
+            pltpu.VMEM((micro * k_rows, depth), BF16),
+            pltpu.VMEM((2, q_rows, half), F32),
+        ]
+        + [pltpu.VMEM((micro, 2, q_rows, half), BF16)] * 4
+        + [dma((4, outer))] * 4
+        + [dma((2, micro))] * 2
+        + [dma((micro,))] * 2,
+        compiler_params=pltpu.CompilerParams(
+            collective_id=0, has_side_effects=True, vmem_limit_bytes=58 << 20
+        ),
+    )(scalars, top, q, k, v, wo, wq, wk, wv)
 
 
 def ranked(marked):
@@ -230,50 +452,56 @@
     q_rows = grad_top.shape[0] // micro
     k_rows = saved_key.shape[1] // micro
     half = grad_top.shape[1] // 2
-    factors = (devices // 2, 2) if devices % 2 == 0 else None
-    wo, sources = gathered(w_out[0], factors)
-    wq, _ = gathered(w_query[0], factors)
-    wk, _ = gathered(w_key[0], factors)
-    wv, _ = gathered(w_value[0], factors)
-    order = jnp.stack(sources).astype(jnp.int32)
-
     mp_swap = [(0, 1), (1, 0)]
-    top = grad_top.reshape(grad_top.shape[0], 2, half).transpose(1, 0, 2)
-    scalars = [
-        jnp.concatenate([order, query_length[s], key_offset[s], key_length[s]])
-        for s in range(micro)
-    ]
-
-    def tick(s, grad, at):
-        return run_tick(
-            scalars[s], grad, at, s, saved_query, saved_key, saved_value, wo, wq, q_rows, k_rows
+    if w_out.shape[2] == BLOCK and devices % 2 == 0 and devices > 4 and micro == 2:
+        table = jnp.concatenate([query_length, key_offset, key_length], axis=1)
+        sections, parts = run_fused(
+            table, grad_top, saved_query, saved_key, saved_value, w_out, w_query, w_key, w_value,
+            devices // 2,
         )
-
-    upper = [tick(s, top, s) for s in range(micro)]
-    upper_half, incoming = [], []
-    for s in range(micro):
-        mixed = upper[s][0]
-        other = lax.ppermute(mixed, "mp", mp_swap)
-        rows = top[:, s * q_rows : (s + 1) * q_rows]
-        section = (rows.astype(F32) + (mixed.astype(F32) + other.astype(F32))).astype(BF16)
-        incoming.append(lax.ppermute(section, "segment", [(1, 0)]))
-        upper_half.append(lax.dynamic_index_in_dim(section, mp, 0, keepdims=False))
-    lower = [tick(s, incoming[s], 0) for s in range(micro)]
-    halves = []
-    for s in range(micro):
-        mixed = lower[s][0]
-        other = lax.ppermute(
-            lax.dynamic_index_in_dim(mixed, 1 - mp, 0, keepdims=False), "mp", mp_swap
-        )
-        own = lax.dynamic_index_in_dim(mixed, mp, 0, keepdims=False)
-        base = lax.dynamic_index_in_dim(incoming[s], mp, 0, keepdims=False)
-        low = (base.astype(F32) + (own.astype(F32) + other.astype(F32))).astype(BF16)
-        halves.append(jnp.where(seg == 1, upper_half[s], low))
-    sections = jnp.concatenate(halves, axis=0)
-
-    kg = jnp.concatenate([jnp.where(seg == 1, upper[s][1], lower[s][1]) for s in range(micro)], 0)
-    vg = jnp.concatenate([jnp.where(seg == 1, upper[s][2], lower[s][2]) for s in range(micro)], 0)
-    parts = run_encoder(order, kg, vg, wk, wv)
+    else:
+        wo, sources = gathered(w_out[0])
+        wq, _ = gathered(w_query[0])
+        wk, _ = gathered(w_key[0])
+        wv, _ = gathered(w_value[0])
+        order = jnp.stack(sources).astype(jnp.int32)
+
+        top = grad_top.reshape(grad_top.shape[0], 2, half).transpose(1, 0, 2)
+        scalars = [
+            jnp.concatenate([order, query_length[s], key_offset[s], key_length[s]])
+            for s in range(micro)
+        ]
+
+        def tick(s, grad, at):
+            return run_tick(
+                scalars[s], grad, at, s, saved_query, saved_key, saved_value, wo, wq, q_rows, k_rows
+            )
+
+        upper = [tick(s, top, s) for s in range(micro)]
+        upper_half, incoming = [], []
+        for s in range(micro):
+            mixed = upper[s][0]
+            other = lax.ppermute(mixed, "mp", mp_swap)
+            rows = top[:, s * q_rows : (s + 1) * q_rows]
+            section = (rows.astype(F32) + (mixed.astype(F32) + other.astype(F32))).astype(BF16)
+            incoming.append(lax.ppermute(section, "segment", [(1, 0)]))
+            upper_half.append(lax.dynamic_index_in_dim(section, mp, 0, keepdims=False))
+        lower = [tick(s, incoming[s], 0) for s in range(micro)]
+        halves = []
+        for s in range(micro):
+            mixed = lower[s][0]
+            other = lax.ppermute(
+                lax.dynamic_index_in_dim(mixed, 1 - mp, 0, keepdims=False), "mp", mp_swap
+            )
+            own = lax.dynamic_index_in_dim(mixed, mp, 0, keepdims=False)
+            base = lax.dynamic_index_in_dim(incoming[s], mp, 0, keepdims=False)
+            low = (base.astype(F32) + (own.astype(F32) + other.astype(F32))).astype(BF16)
+            halves.append(jnp.where(seg == 1, upper_half[s], low))
+        sections = jnp.concatenate(halves, axis=0)[None]
+
+        kg = jnp.concatenate([jnp.where(seg == 1, upper[s][1], lower[s][1]) for s in range(micro)], 0)
+        vg = jnp.concatenate([jnp.where(seg == 1, upper[s][2], lower[s][2]) for s in range(micro)], 0)
+        parts = run_encoder(order, kg, vg, wk, wv)
     away = lax.dynamic_slice_in_dim(parts, (1 - seg) * 2, 2, 0)
     mine = lax.dynamic_slice_in_dim(parts, seg * 2, 2, 0)
     arrived = lax.ppermute(away, "segment", mp_swap)
@@ -330,7 +558,7 @@
     from_left = lax.ppermute(to_right, "dp", forward)
     from_right = lax.ppermute(to_left, "dp", backward)
     owned = small_call(place_kernel, take, [from_left, local, from_right], shape)
-    return sections[None], owned.reshape(tiles * TILE, features)
+    return sections, owned.reshape(tiles * TILE, features)
 
 
 def solution(mesh):

time: 377 us -> 249 us (0.66)
  waiting for transfers between devices: 244 us -> 29.3 us
  Pallas kernels: 55.4 us -> 203 us
  starting transfers between devices: 40.4 us -> 6.36 us
  local copies, waits for them, and re-layouts: 23.7 us -> 4.76 us
  other arithmetic: 11.7 us -> 4.67 us
    ppermute x34 -> x0, waiting for transfers between devices: 226 us -> none  [the longest x12 92.2 us: gathered(): block = lax.ppermute(block, 'dp', ring)]
    pallas_call x5 -> x1, Pallas kernels: 52.8 us -> 200 us  [run_fused(): pl.pallas_call(functools.partial(fused_kernel, (q_rows, k_rows, outer, de...]
    ppermute x34 -> x0, starting transfers between devices: 33.9 us -> none  [the longest x16 19.7 us: gathered(): blocks.append(lax.ppermute(block, 'dp', swap))]
    unnamed x88 -> x6, local copies, waits for them, and re-layouts: 17.4 us -> 1.74 us
    ppermute x1, waiting for transfers between devices: 0.01 us -> 6.19 us  [on_device(): from_left = lax.ppermute(to_right, 'dp', forward)]
    reshape x1 -> x0, local copies, waits for them, and re-layouts: 4.13 us -> none  [on_device(): top = grad_top.reshape(grad_top.shape[0], 2, half).transpose(1, 0, 2)]
  transfers between devices with their start and end apart: 38 -> 4, of which waited for: 28 -> 4; matrix products, arithmetic and copies ran while one was open for 5% -> 0% of each run, Pallas kernels for 8% -> 0%
where the time goes in v3:
time: 249 us
  Pallas kernels  203 us (82%)
  waiting for transfers between devices  29.3 us (12%)
  starting transfers between devices  6.36 us (3%)
  local copies, waits for them, and re-layouts  4.76 us (2%)
  other arithmetic  4.67 us (2%)
    pallas_call x1, Pallas kernels, run_fused(): pl.pallas_call(functools.partial(fused_kernel, (q_rows, k_rows, outer, de...  200 us
    ppermute x1, waiting for transfers between devices, on_device(): lax.ppermute(lax.dynamic_index_in_dim(summed, 1 - mp, 0, keepdims=False),...  17.4 us
    ppermute x1, waiting for transfers between devices, on_device(): from_left = lax.ppermute(to_right, 'dp', forward)  6.19 us
  transfers between devices with their start and end apart: 4, of which 4 were waited for; matrix products, arithmetic and copies ran while one was open for 0% of the time, Pallas kernels for 0%

profile of v3, /device:TPU:0, one launch (start us, length us, event | category | flops | bytes accessed | tf_op | source)
XLA Modules:
  0.0 248.6 jit_solution(12227526203938289501)
XLA Ops:
  0.7 0.8 copy.16
  1.4 0.1 reshape.38
  1.6 0.1 convert_reduce_fusion.2
  1.7 1.5 pad_add_fusion.1
  3.2 200.2 %shard_map.131 = (bf16[1,512,1024]{2,1,0:T(8,128)(2,1)}, bf16[4,768,512]{2,1,0:T(8,128)(2,1)}) custom-call(s32[2,6]{1,0:T(2,128)} %get-tuple-element.22.sc, bf16[512,2048]{1,0:T(8,128)(2,1)} %top_ref.1, bf16[1,512,1024]{2,1,0:T(8,128)(2,1)} %q_ref.1, bf16[1,768,1024]{2,1,0:T(8,128)(2,1)} %k_ref.1, bf16[1,768,1024]{2,1,0:T(8,128)(2,1)} %v_ref.1, ...), custom_call_target="tpu_custom_call" | custom-call | tf_op jit(solution)/shard_map/pallas_call | solution.py:403
  203.4 0.0 copy-start
  203.4 2.8 %constant_dynamic-slice_fusion.1 = bf16[2,768,512]{2,1,0:T(8,128)(2,1)} fusion(bf16[4,768,512]{2,1,0:T(8,128)(2,1)} %get-tuple-element.8, s32[]{:T(128)S(6)} %select_n.129), kind=kLoop, calls=%fused_computation.44 | loop fusion | bytes 3145732 | tf_op jit(solution)/shard_map/dynamic_slice | solution.py:505
  206.2 0.0 collective-permute-start
  206.3 0.1 convert_reduce_fusion.1
  206.4 0.1 convert_reduce_fusion
  206.5 3.5 %collective-permute-done = bf16[2,768,512]{2,1,0:T(8,128)(2,1)} collective-permute-done((bf16[2,768,512]{2,1,0:T(8,128)(2,1)}, bf16[2,768,512]{2,1,0:T(8,128)(2,1)}, u32[]{:S(2)}, u32[]{:S(2)}) %collective-permute-start) | collective-permute-done | bytes 1572896 | tf_op jit(solution)/shard_map/ppermute | solution.py:507
  210.0 0.0 copy-done
  210.0 1.8 add_convert_fusion
  211.8 0.1 dynamic-slice_bitcast_fusion
  212.0 1.6 collective-permute-start.1
  213.6 0.1 fusion.6
  213.7 0.1 pad_add_fusion.3.sc
  213.8 0.1 convert_reduce_fusion.3
  213.9 0.1 select_reduce_fusion.2
  214.1 0.2 fusion.8
  214.2 17.4 %collective-permute-done.1 = bf16[768,512]{1,0:T(8,128)(2,1)S(1)} collective-permute-done((bf16[768,512]{1,0:T(8,128)(2,1)S(1)}, bf16[768,512]{1,0:T(8,128)(2,1)S(1)}, u32[]{:S(2)}, u32[]{:S(2)}) %collective-permute-start.1) | collective-permute-done | bytes 786464 | tf_op jit(solution)/shard_map/ppermute | solution.py:509
  231.6 0.0 copy-start.1
  231.6 1.0 shard_map.132
  232.6 0.6 collective-permute-start.2
  233.2 4.2 %collective-permute-start.3 = (bf16[2,128,512]{2,1,0:T(8,128)(2,1)S(1)}, bf16[2,128,512]{2,1,0:T(8,128)(2,1)S(1)}, u32[]{:S(2)}, u32[]{:S(2)}) collective-permute-start(bf16[2,128,512]{2,1,0:T(8,128)(2,1)S(1)} %get-tuple-element.11), channel_id=1, source_target_pairs={{2,0},{4,2},{6,4},{8,6},{10,8},{12,10},{14,12},{0,14},{3,1},{5,3},... | collective-permute-start | bytes 786440 | tf_op jit(solution)/shard_map/ppermute | solution.py:559
  237.4 0.1 pad_add_fusion.2
  237.5 0.1 pad_add_fusion
  237.5 0.1 select_reduce_fusion.sc
  237.7 6.2 %collective-permute-done.2.left_ref = bf16[2,128,512]{2,1,0:T(8,128)(2,1)S(1)} collective-permute-done((bf16[2,128,512]{2,1,0:T(8,128)(2,1)S(1)}, bf16[2,128,512]{2,1,0:T(8,128)(2,1)S(1)}, u32[]{:S(2)}, u32[]{:S(2)}) %collective-permute-start.2) | collective-permute-done | bytes 262176 | tf_op jit(solution)/shard_map/ppermute | solution.py:558
  243.8 2.2 collective-permute-done.3.right_ref
  246.0 1.6 shard_map.133
  247.6 0.0 copy-done.1
  247.6 1.0 copy.18
  (9 shorter events, 0.1 us)
Async XLA Ops:
  203.4 6.6 %copy-start = (bf16[4,768,512]{2,1,0:T(8,128)(2,1)S(1)}, bf16[4,768,512]{2,1,0:T(8,128)(2,1)}, u32[]{:S(2)}) copy-start(bf16[4,768,512]{2,1,0:T(8,128)(2,1)} %get-tuple-element.8) | copy-start | bytes 9437188
  206.2 3.8 %collective-permute-start = (bf16[2,768,512]{2,1,0:T(8,128)(2,1)}, bf16[2,768,512]{2,1,0:T(8,128)(2,1)}, u32[]{:S(2)}, u32[]{:S(2)}) collective-permute-start(bf16[2,768,512]{2,1,0:T(8,128)(2,1)} %constant_dynamic-slice_fusion.1), channel_id=1, source_target_pairs={{0,16},{16,0},{1,17},{17,1},{2,18},{18,2},{3,19},{19,3},{4,20},{20... | collective-permute-start | bytes 4718600 | tf_op jit(solution)/shard_map/ppermute | solution.py:507
  212.0 19.6 %collective-permute-start.1 = (bf16[768,512]{1,0:T(8,128)(2,1)S(1)}, bf16[768,512]{1,0:T(8,128)(2,1)S(1)}, u32[]{:S(2)}, u32[]{:S(2)}) collective-permute-start(bf16[768,512]{1,0:T(8,128)(2,1)S(1)} %get-tuple-element.14), channel_id=1, source_target_pairs={{0,1},{1,0},{2,3},{3,2},{4,5},{5,4},{6,7},{7,6},{8,9},{9,8},{10,11... | collective-permute-start | bytes 2359304 | tf_op jit(solution)/shard_map/ppermute | solution.py:509
  231.6 16.0 %copy-start.1 = (bf16[1,512,1024]{2,1,0:T(8,128)(2,1)S(1)}, bf16[1,512,1024]{2,1,0:T(8,128)(2,1)}, u32[]{:S(2)}) copy-start(bf16[1,512,1024]{2,1,0:T(8,128)(2,1)} %get-tuple-element.28) | copy-start | bytes 3145732
  232.6 11.2 %collective-permute-start.2 = (bf16[2,128,512]{2,1,0:T(8,128)(2,1)S(1)}, bf16[2,128,512]{2,1,0:T(8,128)(2,1)S(1)}, u32[]{:S(2)}, u32[]{:S(2)}) collective-permute-start(bf16[2,128,512]{2,1,0:T(8,128)(2,1)S(1)} %get-tuple-element.9), channel_id=1, source_target_pairs={{0,2},{2,4},{4,6},{6,8},{8,10},{10,12},{12,14},{14,0},{1,3},{3,5},... | collective-permute-start | bytes 786440 | tf_op jit(solution)/shard_map/ppermute | solution.py:558
  233.2 12.9 %collective-permute-start.3 = (bf16[2,128,512]{2,1,0:T(8,128)(2,1)S(1)}, bf16[2,128,512]{2,1,0:T(8,128)(2,1)S(1)}, u32[]{:S(2)}, u32[]{:S(2)}) collective-permute-start(bf16[2,128,512]{2,1,0:T(8,128)(2,1)S(1)} %get-tuple-element.11), channel_id=1, source_target_pairs={{2,0},{4,2},{6,4},{8,6},{10,8},{12,10},{14,12},{0,14},{3,1},{5,3},... | collective-permute-start | bytes 786440 | tf_op jit(solution)/shard_map/ppermute | solution.py:559

commit v4 on v3

--- a/solution.py
+++ b/solution.py
@@ -142,8 +142,7 @@
     )(scalars, kg, vg, *wk, *wv)
 
 
-def pick_kernel(sc, own_ref, other_ref, local_ref, left_ref, right_ref):
-    local_ref[...] = (own_ref[...].astype(F32) + other_ref[...].astype(F32)).astype(BF16)
+def pick_kernel(sc, local_ref, left_ref, right_ref):
     for c in range(CAP):
         left_ref[c] = local_ref[sc[c]]
         right_ref[c] = local_ref[sc[CAP + c]]
@@ -186,8 +185,9 @@
 
 
 def fused_kernel(dims, sc, top_ref, q_ref, k_ref, v_ref, wo_ref, wq_ref, wk_ref, wv_ref,
-                 sections_ref, parts_ref, wbuf, kg, vg, acc, mixed, other, section, incoming,
-                 zs, zr, xs, xr, ms, mr, ss, sr):
+                 sections_ref, local_ref, wbuf, kg, vg, acc, mixed, other, section, incoming,
+                 parts, arrived, summed, crossed,
+                 zs, zr, xs, xr, ms, mr, ss, sr, es, er, ps, pr, ys, yr):
     q_rows, k_rows, outer, heads = dims
     half = acc.shape[2]
     per = half // BLOCK
@@ -219,8 +219,24 @@
     def z_copy(w, r):
         return send(block(w, r, 0), block(w, r + 1, 0), zs.at[w, r], zr.at[w, r], (seg, up, mp))
 
+    last = outer - 1
+    depth = kg.shape[1]
+    upper_rows, lower_rows = pl.ds(0, depth // 2), pl.ds(depth // 2, depth // 2)
+
     def x_copy(w, r):
-        return send(block(w, r, 0), block(w, r, 1), xs.at[w, r], xr.at[w, r], (seg, side, mp))
+        src, dst = block(w, r, 0), block(w, r, 1)
+        if r == last:
+            src, dst = src.at[upper_rows], dst.at[upper_rows]
+        return send(src, dst, xs.at[w, r], xr.at[w, r], (seg, side, mp))
+
+    def extra_copy(w):
+        src, dst = block(w, last - 1, 1).at[lower_rows], block(w, last, 1).at[lower_rows]
+        return send(src, dst, es.at[w], er.at[w], (seg, up, mp))
+
+    def extras(pair):
+        for w in pair:
+            x_copy(w, last - 1).wait_recv()
+            extra_copy(w).start()
 
     def advance(pair, r):
         for w in pair:
@@ -230,10 +246,12 @@
                 z_copy(w, r).start()
             x_copy(w, r).start()
 
-    def arrive(pair):
+    def arrive(pair, r):
         for w in pair:
-            for r in range(outer):
+            if r != last - 1:
                 x_copy(w, r).wait_recv()
+            if r == last:
+                extra_copy(w).wait_recv()
 
     slots = [(r, sx) for r in range(outer) for sx in range(2)]
 
@@ -319,8 +337,10 @@
 
     for r in range(outer):
         advance((0, 1), r)
+    extras((0, 1))
     advance((2, 3), 0)
-    arrive((0, 1))
+    for r in range(outer):
+        arrive((0, 1), r)
 
     @pl.when(seg == 1)
     def _():
@@ -348,7 +368,8 @@
         tick(0, incoming_block(0))
         lower_copy(0).start()
 
-    advance((2, 3), outer - 1)
+    advance((2, 3), last)
+    extras((2, 3))
 
     @pl.when(seg == 0)
     def _():
@@ -357,26 +378,71 @@
         lower_copy(1).start()
         finish_lower(0)
 
-    arrive((2, 3))
-    quarter = parts_ref.shape[2]
     step = 256
 
-    def encode(i, carry):
-        rows = pl.ds(pl.multiple_of(i * step, step), step)
-        for r, sx in slots:
-            src = source(r, sx)
-            each = quarter // BLOCK
-            at = pl.ds(pl.multiple_of((src % each) * BLOCK, BLOCK), BLOCK)
-            part = dot(kg[rows, :], block(2, r, sx)[...], 1, 0)
-            part += dot(vg[rows, :], block(3, r, sx)[...], 1, 0)
-            parts_ref[src // each, rows, at] = part.astype(BF16)
-        return carry
-
-    lax.fori_loop(0, kg.shape[0] // step, encode, 0)
+    def quarter_of(r):
+        return (z + outer - r) % outer
+
+    def part_copy(r):
+        q = quarter_of(r)
+        return send(parts.at[q], arrived.at[q % 2], ps.at[r], pr.at[r], (1 - seg, me, mp))
+
+    def cross_copy(r):
+        return send(summed.at[quarter_of(r) % 2], crossed, ys.at[0], yr.at[0], (seg, me, 1 - mp))
+
+    def encode(r):
+        q = quarter_of(r)
+
+        def rows_step(i, carry):
+            rows = pl.ds(pl.multiple_of(i * step, step), step)
+            for sx in range(2):
+                at = pl.ds(pl.multiple_of((x if sx == 0 else 1 - x) * BLOCK, BLOCK), BLOCK)
+                part = dot(kg[rows, :], block(2, r, sx)[...], 1, 0)
+                part += dot(vg[rows, :], block(3, r, sx)[...], 1, 0)
+                parts[q, rows, at] = part.astype(BF16)
+            return carry
+
+        lax.fori_loop(0, kg.shape[0] // step, rows_step, 0)
+
+        @pl.when(seg != q // 2)
+        def _():
+            part_copy(r).start()
+
+    def reduce(r):
+        q = quarter_of(r)
+
+        @pl.when(seg == q // 2)
+        def _():
+            part_copy(r).wait_recv()
+            summed[q % 2] = (parts[q].astype(F32) + arrived[q % 2].astype(F32)).astype(BF16)
+
+            @pl.when(mp != q % 2)
+            def _():
+                cross_copy(r).start()
+
+    for r in range(outer):
+        if r == last:
+
+            @pl.when(seg == 0)
+            def _():
+                finish_lower(1)
+
+        arrive((2, 3), r)
+        encode(r)
+        if r > 0:
+            reduce(r - 1)
+    reduce(last)
+    cross_copy(0).wait_recv()
+    local_ref[...] = (summed[mp].astype(F32) + crossed[...].astype(F32)).astype(BF16)
+    cross_copy(0).wait_send()
+    for r in range(outer):
+
+        @pl.when(seg != quarter_of(r) // 2)
+        def _():
+            part_copy(r).wait_send()
 
     @pl.when(seg == 0)
     def _():
-        finish_lower(1)
         for s in range(2):
             lower_copy(s).wait_send()
 
@@ -389,6 +455,8 @@
     for w in range(4):
         for r in range(outer):
             x_copy(w, r).wait_send()
+            if r == last:
+                extra_copy(w).wait_send()
             if r < outer - 1:
                 z_copy(w, r).wait_send()
 
@@ -406,7 +474,7 @@
         out_specs=[vmem, vmem],
         out_shape=[
             jax.ShapeDtypeStruct((1, micro * q_rows, half), BF16),
-            jax.ShapeDtypeStruct((4, micro * k_rows, width // 4), BF16),
+            jax.ShapeDtypeStruct((micro * k_rows, width // 4), BF16),
         ],
         scratch_shapes=[
             pltpu.VMEM((4, 2 * outer, depth, BLOCK), BF16),
@@ -415,9 +483,14 @@
             pltpu.VMEM((2, q_rows, half), F32),
         ]
         + [pltpu.VMEM((micro, 2, q_rows, half), BF16)] * 4
+        + [pltpu.VMEM((n, micro * k_rows, width // 4), BF16) for n in (4, 2, 2)]
+        + [pltpu.VMEM((micro * k_rows, width // 4), BF16)]
         + [dma((4, outer))] * 4
         + [dma((2, micro))] * 2
-        + [dma((micro,))] * 2,
+        + [dma((micro,))] * 2
+        + [dma((4,))] * 2
+        + [dma((outer,))] * 2
+        + [dma((1,))] * 2,
         compiler_params=pltpu.CompilerParams(
             collective_id=0, has_side_effects=True, vmem_limit_bytes=58 << 20
         ),
@@ -453,9 +526,9 @@
     k_rows = saved_key.shape[1] // micro
     half = grad_top.shape[1] // 2
     mp_swap = [(0, 1), (1, 0)]
-    if w_out.shape[2] == BLOCK and devices % 2 == 0 and devices > 4 and micro == 2:
+    if w_out.shape[2] == BLOCK and devices == 8 and micro == 2:
         table = jnp.concatenate([query_length, key_offset, key_length], axis=1)
-        sections, parts = run_fused(
+        sections, kept = run_fused(
             table, grad_top, saved_query, saved_key, saved_value, w_out, w_query, w_key, w_value,
             devices // 2,
         )
@@ -502,14 +575,15 @@
         kg = jnp.concatenate([jnp.where(seg == 1, upper[s][1], lower[s][1]) for s in range(micro)], 0)
         vg = jnp.concatenate([jnp.where(seg == 1, upper[s][2], lower[s][2]) for s in range(micro)], 0)
         parts = run_encoder(order, kg, vg, wk, wv)
-    away = lax.dynamic_slice_in_dim(parts, (1 - seg) * 2, 2, 0)
-    mine = lax.dynamic_slice_in_dim(parts, seg * 2, 2, 0)
-    arrived = lax.ppermute(away, "segment", mp_swap)
-    summed = (mine.astype(F32) + arrived.astype(F32)).astype(BF16)
-    crossing = lax.ppermute(
-        lax.dynamic_index_in_dim(summed, 1 - mp, 0, keepdims=False), "mp", mp_swap
-    )
-    kept = lax.dynamic_index_in_dim(summed, mp, 0, keepdims=False)
+        away = lax.dynamic_slice_in_dim(parts, (1 - seg) * 2, 2, 0)
+        mine = lax.dynamic_slice_in_dim(parts, seg * 2, 2, 0)
+        arrived = lax.ppermute(away, "segment", mp_swap)
+        summed = (mine.astype(F32) + arrived.astype(F32)).astype(BF16)
+        crossing = lax.ppermute(
+            lax.dynamic_index_in_dim(summed, 1 - mp, 0, keepdims=False), "mp", mp_swap
+        )
+        kept = lax.dynamic_index_in_dim(summed, mp, 0, keepdims=False)
+        kept = (kept.astype(F32) + crossing.astype(F32)).astype(BF16)
 
     tiles = kept.shape[0] // TILE
     features = kept.shape[1]
@@ -547,11 +621,9 @@
     tiled = (tiles, TILE, features)
     shape = jax.ShapeDtypeStruct(tiled, BF16)
     handed = jax.ShapeDtypeStruct((CAP, TILE, features), BF16)
-    local, to_left, to_right = small_call(
-        pick_kernel,
-        jnp.concatenate([send_left, send_right]),
-        [kept.reshape(tiled), crossing.reshape(tiled)],
-        [shape, handed, handed],
+    local = kept.reshape(tiled)
+    to_left, to_right = small_call(
+        pick_kernel, jnp.concatenate([send_left, send_right]), [local], [handed, handed]
     )
     forward = [(i, (i + 1) % devices) for i in range(devices)]
     backward = [(b, a) for a, b in forward]

time: 249 us -> 214 us (0.86)
  waiting for transfers between devices: 29.3 us -> 9.12 us
  Pallas kernels: 203 us -> 193 us
    ppermute x2 -> x0, waiting for transfers between devices: 20.9 us -> none  [the longest x1 17.4 us: on_device(): lax.ppermute(lax.dynamic_index_in_dim(summed, 1 - mp, 0, keepdims=False),...]
    pallas_call x1, Pallas kernels: 200 us -> 191 us  [run_fused(): pl.pallas_call(functools.partial(fused_kernel, (q_rows, k_rows, outer, de...]
    dynamic_slice x1 -> x0, local copies, waits for them, and re-layouts: 2.84 us -> none  [on_device(): away = lax.dynamic_slice_in_dim(parts, (1 - seg) * 2, 2, 0)]
  transfers between devices with their start and end apart: 4 -> 2, of which waited for: 4 -> 2; matrix products, arithmetic and copies ran while one was open for 0% -> 0% of each run, Pallas kernels for 0% -> 0%
where the time goes in v4:
time: 214 us; the launch traced here: 213 us
  Pallas kernels  193 us (90%)
  waiting for transfers between devices  9.12 us (4%)
  starting transfers between devices  4.78 us (2%)
  local copies, waits for them, and re-layouts  2.93 us (1%)
  other arithmetic  2.77 us (1%)
    pallas_call x1, Pallas kernels, run_fused(): pl.pallas_call(functools.partial(fused_kernel, (q_rows, k_rows, outer, de...  191 us
    ppermute x1, waiting for transfers between devices, on_device(): from_left = lax.ppermute(to_right, 'dp', forward)  7.41 us
  transfers between devices with their start and end apart: 2, of which 2 were waited for; matrix products, arithmetic and copies ran while one was open for 0% of the time, Pallas kernels for 0%

profile of v4, /device:TPU:0, one launch (start us, length us, event | category | flops | bytes accessed | tf_op | source)
XLA Modules:
  0.0 213.1 jit_solution(16860278156217913376)
XLA Ops:
  0.7 0.8 copy.16
  1.4 0.1 reshape.34
  1.5 0.1 convert_reduce_fusion
  1.7 0.1 convert_reduce_fusion.1
  1.8 0.2 fusion.6
  2.0 0.1 pad_add_fusion.3.sc
  2.0 1.4 pad_add_fusion.1.sc
  3.4 190.6 %shard_map.131 = (bf16[1,512,1024]{2,1,0:T(8,128)(2,1)}, bf16[768,512]{1,0:T(8,128)(2,1)}) custom-call(s32[2,6]{1,0:T(2,128)} %pad_add_fusion.1.sc, bf16[512,2048]{1,0:T(8,128)(2,1)} %top_ref.1, bf16[1,512,1024]{2,1,0:T(8,128)(2,1)} %q_ref.1, bf16[1,768,1024]{2,1,0:T(8,128)(2,1)} %k_ref.1, bf16[1,768,1024]{2,1,0:T(8,128)(2,1)} %v_ref.1, ...), custom_call_target="tpu_custom_call" | custom-call | tf_op jit(solution)/shard_map/pallas_call | solution.py:471
  194.0 0.0 copy-start
  194.0 1.1 copy-done
  195.1 0.0 copy-start.1
  195.2 0.6 shard_map.132
  195.7 1.1 collective-permute-start
  196.9 3.7 %collective-permute-start.1 = (bf16[2,128,512]{2,1,0:T(8,128)(2,1)S(1)}, bf16[2,128,512]{2,1,0:T(8,128)(2,1)S(1)}, u32[]{:S(2)}, u32[]{:S(2)}) collective-permute-start(bf16[2,128,512]{2,1,0:T(8,128)(2,1)S(1)} %get-tuple-element.9), channel_id=1, source_target_pairs={{2,0},{4,2},{6,4},{8,6},{10,8},{12,10},{14,12},{0,14},{3,1},{5,3},... | collective-permute-start | bytes 786440 | tf_op jit(solution)/shard_map/ppermute | solution.py:631
  200.6 0.1 convert_reduce_fusion.2
  200.7 0.1 convert_reduce_fusion.3
  200.8 0.2 fusion.8
  201.0 0.2 select_reduce_fusion.1
  201.1 0.1 pad_add_fusion
  201.2 0.1 pad_add_fusion.2
  201.3 0.1 select_reduce_fusion.sc
  201.4 7.4 %collective-permute-done.left_ref = bf16[2,128,512]{2,1,0:T(8,128)(2,1)S(1)} collective-permute-done((bf16[2,128,512]{2,1,0:T(8,128)(2,1)S(1)}, bf16[2,128,512]{2,1,0:T(8,128)(2,1)S(1)}, u32[]{:S(2)}, u32[]{:S(2)}) %collective-permute-start) | collective-permute-done | bytes 262176 | tf_op jit(solution)/shard_map/ppermute | solution.py:630
  208.8 1.7 collective-permute-done.1.right_ref
  210.6 1.6 shard_map.133
  212.1 0.0 copy-done.1
  212.1 1.0 copy.18
  (9 shorter events, 0.1 us)
Async XLA Ops:
  194.0 1.1 copy-start
  195.1 17.0 %copy-start.1 = (bf16[1,512,1024]{2,1,0:T(8,128)(2,1)S(1)}, bf16[1,512,1024]{2,1,0:T(8,128)(2,1)}, u32[]{:S(2)}) copy-start(bf16[1,512,1024]{2,1,0:T(8,128)(2,1)} %get-tuple-element.24) | copy-start | bytes 3145732
  195.7 13.1 %collective-permute-start = (bf16[2,128,512]{2,1,0:T(8,128)(2,1)S(1)}, bf16[2,128,512]{2,1,0:T(8,128)(2,1)S(1)}, u32[]{:S(2)}, u32[]{:S(2)}) collective-permute-start(bf16[2,128,512]{2,1,0:T(8,128)(2,1)S(1)} %get-tuple-element.8), channel_id=1, source_target_pairs={{0,2},{2,4},{4,6},{6,8},{8,10},{10,12},{12,14},{14,0},{1,3},{3,5},... | collective-permute-start | bytes 786440 | tf_op jit(solution)/shard_map/ppermute | solution.py:630
  196.9 13.7 %collective-permute-start.1 = (bf16[2,128,512]{2,1,0:T(8,128)(2,1)S(1)}, bf16[2,128,512]{2,1,0:T(8,128)(2,1)S(1)}, u32[]{:S(2)}, u32[]{:S(2)}) collective-permute-start(bf16[2,128,512]{2,1,0:T(8,128)(2,1)S(1)} %get-tuple-element.9), channel_id=1, source_target_pairs={{2,0},{4,2},{6,4},{8,6},{10,8},{12,10},{14,12},{0,14},{3,1},{5,3},... | collective-permute-start | bytes 786440 | tf_op jit(solution)/shard_map/ppermute | solution.py:631

commit v5 on v4

--- a/solution.py
+++ b/solution.py
@@ -368,8 +368,6 @@
         tick(0, incoming_block(0))
         lower_copy(0).start()
 
-    advance((2, 3), last)
-    extras((2, 3))
 
     @pl.when(seg == 0)
     def _():
@@ -378,6 +376,7 @@
         lower_copy(1).start()
         finish_lower(0)
 
+    advance((2, 3), last)
     step = 256
 
     def quarter_of(r):
@@ -429,7 +428,9 @@
 
         arrive((2, 3), r)
         encode(r)
-        if r > 0:
+        if r == 0:
+            extras((2, 3))
+        else:
             reduce(r - 1)
     reduce(last)
     cross_copy(0).wait_recv()

time: 214 us -> 208 us (0.972)
  Pallas kernels: 193 us -> 186 us
    pallas_call x1, Pallas kernels: 191 us -> 184 us  [run_fused(): pl.pallas_call(functools.partial(fused_kernel, (q_rows, k_rows, outer, de...]
where the time goes in v5:
time: 208 us; the launch traced here: 207 us
  Pallas kernels  186 us (89%)
  waiting for transfers between devices  9.28 us (4%)
  starting transfers between devices  5.85 us (3%)
  local copies, waits for them, and re-layouts  2.93 us (1%)
  other arithmetic  2.77 us (1%)
    pallas_call x1, Pallas kernels, run_fused(): pl.pallas_call(functools.partial(fused_kernel, (q_rows, k_rows, outer, de...  184 us
    ppermute x1, waiting for transfers between devices, on_device(): from_left = lax.ppermute(to_right, 'dp', forward)  5.69 us
    ppermute x1, starting transfers between devices, on_device(): from_right = lax.ppermute(to_left, 'dp', backward)  4.3 us
  transfers between devices with their start and end apart: 2, of which 2 were waited for; matrix products, arithmetic and copies ran while one was open for 0% of the time, Pallas kernels for 0%

profile of v5, /device:TPU:0, one launch (start us, length us, event | category | flops | bytes accessed | tf_op | source)
XLA Modules:
  0.0 207.5 jit_solution(205840470704359809)
XLA Ops:
  0.7 0.8 copy.16
  1.4 0.1 reshape.34
  1.5 0.1 convert_reduce_fusion
  1.7 0.1 convert_reduce_fusion.1
  1.8 0.2 fusion.6
  2.0 0.1 pad_add_fusion.3.sc
  2.0 1.4 pad_add_fusion.1.sc
  3.4 183.8 %shard_map.131 = (bf16[1,512,1024]{2,1,0:T(8,128)(2,1)}, bf16[768,512]{1,0:T(8,128)(2,1)}) custom-call(s32[2,6]{1,0:T(2,128)} %pad_add_fusion.1.sc, bf16[512,2048]{1,0:T(8,128)(2,1)} %top_ref.1, bf16[1,512,1024]{2,1,0:T(8,128)(2,1)} %q_ref.1, bf16[1,768,1024]{2,1,0:T(8,128)(2,1)} %k_ref.1, bf16[1,768,1024]{2,1,0:T(8,128)(2,1)} %v_ref.1, ...), custom_call_target="tpu_custom_call" | custom-call | tf_op jit(solution)/shard_map/pallas_call | solution.py:472
  187.2 0.0 copy-start
  187.2 1.1 copy-done
  188.3 0.0 copy-start.1
  188.3 0.6 shard_map.132
  188.9 1.5 collective-permute-start
  190.4 4.3 %collective-permute-start.1 = (bf16[2,128,512]{2,1,0:T(8,128)(2,1)S(1)}, bf16[2,128,512]{2,1,0:T(8,128)(2,1)S(1)}, u32[]{:S(2)}, u32[]{:S(2)}) collective-permute-start(bf16[2,128,512]{2,1,0:T(8,128)(2,1)S(1)} %get-tuple-element.9), channel_id=1, source_target_pairs={{2,0},{4,2},{6,4},{8,6},{10,8},{12,10},{14,12},{0,14},{3,1},{5,3},... | collective-permute-start | bytes 786440 | tf_op jit(solution)/shard_map/ppermute | solution.py:632
  194.8 0.1 convert_reduce_fusion.2
  194.9 0.1 convert_reduce_fusion.3
  195.1 0.2 fusion.8
  195.2 0.2 select_reduce_fusion.1
  195.4 0.1 pad_add_fusion
  195.5 0.1 pad_add_fusion.2
  195.5 0.1 select_reduce_fusion.sc
  195.7 5.7 %collective-permute-done.left_ref = bf16[2,128,512]{2,1,0:T(8,128)(2,1)S(1)} collective-permute-done((bf16[2,128,512]{2,1,0:T(8,128)(2,1)S(1)}, bf16[2,128,512]{2,1,0:T(8,128)(2,1)S(1)}, u32[]{:S(2)}, u32[]{:S(2)}) %collective-permute-start) | collective-permute-done | bytes 262176 | tf_op jit(solution)/shard_map/ppermute | solution.py:631
  201.3 3.6 %collective-permute-done.1.right_ref = bf16[2,128,512]{2,1,0:T(8,128)(2,1)S(1)} collective-permute-done((bf16[2,128,512]{2,1,0:T(8,128)(2,1)S(1)}, bf16[2,128,512]{2,1,0:T(8,128)(2,1)S(1)}, u32[]{:S(2)}, u32[]{:S(2)}) %collective-permute-start.1) | collective-permute-done | bytes 262176 | tf_op jit(solution)/shard_map/ppermute | solution.py:632
  204.9 1.6 shard_map.133
  206.5 0.0 copy-done.1
  206.5 1.0 copy.18
  (9 shorter events, 0.1 us)
Async XLA Ops:
  187.2 1.1 copy-start
  188.3 18.2 %copy-start.1 = (bf16[1,512,1024]{2,1,0:T(8,128)(2,1)S(1)}, bf16[1,512,1024]{2,1,0:T(8,128)(2,1)}, u32[]{:S(2)}) copy-start(bf16[1,512,1024]{2,1,0:T(8,128)(2,1)} %get-tuple-element.24) | copy-start | bytes 3145732
  188.9 12.5 %collective-permute-start = (bf16[2,128,512]{2,1,0:T(8,128)(2,1)S(1)}, bf16[2,128,512]{2,1,0:T(8,128)(2,1)S(1)}, u32[]{:S(2)}, u32[]{:S(2)}) collective-permute-start(bf16[2,128,512]{2,1,0:T(8,128)(2,1)S(1)} %get-tuple-element.8), channel_id=1, source_target_pairs={{0,2},{2,4},{4,6},{6,8},{8,10},{10,12},{12,14},{14,0},{1,3},{3,5},... | collective-permute-start | bytes 786440 | tf_op jit(solution)/shard_map/ppermute | solution.py:631
  190.4 14.5 %collective-permute-start.1 = (bf16[2,128,512]{2,1,0:T(8,128)(2,1)S(1)}, bf16[2,128,512]{2,1,0:T(8,128)(2,1)S(1)}, u32[]{:S(2)}, u32[]{:S(2)}) collective-permute-start(bf16[2,128,512]{2,1,0:T(8,128)(2,1)S(1)} %get-tuple-element.9), channel_id=1, source_target_pairs={{2,0},{4,2},{6,4},{8,6},{10,8},{12,10},{14,12},{0,14},{3,1},{5,3},... | collective-permute-start | bytes 786440 | tf_op jit(solution)/shard_map/ppermute | solution.py:632
